TPU v7x, 256 devices: a whole 4x4x8 slice. The times are simulated.
256 devices in a mesh: dp: 16 (over y, x), expert: 16 (over z, core).
Axes of the slice: x: 4, y: 4, z: 8, core: 2. Of those that a mesh axis runs over, the one named last changes fastest.
Arguments:
- tokens: bfloat16 [4096, 4096], P('dp', 'expert'), may hold values from -6 to 6
- out_grads: bfloat16 [4096, 4096], P('dp', 'expert'), may hold values from -6 to 6
- routes: int32 [4096, 2], P('dp'), may hold values from 0 to 15, all different within a row; in each aligned block of 256 rows (0 to 255, 256 to 511, ...) at most 64 rows name the same one
- gate_codes: int32 [4096, 2], P('dp'), may hold values from 256 to 4095
- w_gate: bfloat16 [16, 4096, 6400], P('expert', None, 'dp'), may hold values from -0.09375 to 0.09375
- w_up: bfloat16 [16, 4096, 6400], P('expert', None, 'dp'), may hold values from -0.09375 to 0.09375
- w_down: bfloat16 [16, 6400, 4096], P('expert', 'dp'), may hold values from -0.078125 to 0.078125
- proj_in: bfloat16 [4096, 128], replicated, may hold values from -0.09375 to 0.09375
- proj_hidden: bfloat16 [6400, 192], P('dp'), may hold values from -0.078125 to 0.078125
Outputs:
- projected: float32 [16, 16, 12288], P(None, 'expert', 'dp')
Inputs may be any that keep to these rules, and one draw needn't show every extreme that they name: `routes`: each row names 2 different experts. Among the rows of one sequence no expert is named more than 64 times, a bound that some block reaches.
All inputs are finite; a program needn't handle non-finite values.
Results may differ from a plain program's by a relative error of at most 0.0029.
Values may be sent and summed in bfloat16 or wider, within the bound.
No kernel may reach another device: no remote copies, remote signals or barrier semaphores. Data moves between devices by JAX's collectives and lax.ppermute only.
A program may use at most 128 MiB of HBM per device.

v0:
```python
import jax
import jax.numpy as jnp
from jax import lax
from jax.experimental import pallas as pl
from jax.experimental.pallas import tpu as pltpu
from jax.sharding import PartitionSpec as P

SIDE = 4
ROWS = 16
LANES = 128
DEPTH = 1024
F32 = jnp.float32
BF16 = jnp.bfloat16


def place_rows(route_rows, code_rows, n_exp, cap, mine):
    count = route_rows.shape[0]
    flat = route_rows.reshape(-1)
    pairs = flat.shape[0]
    expert_ids = jnp.arange(n_exp, dtype=jnp.int32)
    hits = (flat[:, None] == expert_ids[None, :]).astype(F32)
    earlier = (jnp.arange(pairs)[None, :] < jnp.arange(pairs)[:, None]).astype(F32)
    before = jnp.dot(earlier, hits, preferred_element_type=F32)
    place = jnp.sum(hits * before, axis=1).astype(jnp.int32)
    slot = jnp.arange(n_exp * cap, dtype=jnp.int32)
    target = (flat * cap + place).reshape(count, -1)
    picks = (slot[:, None] == target[:, 0][None, :]) | (slot[:, None] == target[:, 1][None, :])
    own = mine * cap + jnp.arange(cap, dtype=jnp.int32)
    codes = jnp.sum(
        jnp.where(own[:, None] == target.reshape(-1)[None, :], code_rows.reshape(-1)[None, :], 0), axis=1
    )
    return picks.astype(BF16), codes


def dot_t(rows, columns):
    return lax.dot_general(rows, columns, (((1,), (1,)), ((), ())), preferred_element_type=F32)


def step_kernel(sources, n_bufs, first, me_ref, *refs):
    rest = refs[3 * n_bufs :]
    wg, wu, wd, pin, phid = rest[:5]
    acc_in = None if first else rest[5]
    acc_out, gate, upper, back, left, right, turn = rest[5 if first else 6 :]
    k = pl.program_id(0)

    def side(which):
        parts = [refs[3 * i + which][s : s + c] for _, parts in sources for i, s, c in parts]
        return jnp.concatenate([p.reshape(p.shape[0] * ROWS, p.shape[2]) for p in parts], axis=0)

    xs = side(0)
    dys = side(1)
    terms = (
        (gate, lambda: dot_t(xs, wg[0])),
        (upper, lambda: dot_t(xs, wu[0])),
        (back, lambda: dot_t(dys, wd[0])),
        (left, lambda: jnp.dot(xs, pin[...], preferred_element_type=F32)),
        (right, lambda: jnp.dot(dys, pin[...], preferred_element_type=F32)),
    )

    @pl.when(k == 0)
    def _():
        for ref, term in terms:
            ref[...] = term()

    @pl.when(k > 0)
    def _():
        for ref, term in terms:
            ref[...] += term()

    @pl.when(k == pl.num_programs(0) - 1)
    def _():
        codes = side(2).astype(F32)
        weight = (codes[:, 0:1] * 16.0 + codes[:, 1:2]) / 4096.0
        g = gate[...]
        u = upper[...]
        sig = jax.nn.sigmoid(g)
        act = g * sig
        hidden = (act * u).astype(BF16)
        b = back[...] * weight
        d_up = (b * act).astype(BF16)
        d_gate = (b * u * sig * (1.0 + g * (1.0 - sig))).astype(BF16)
        hid = dot_t(hidden, phid[...])
        dgp = dot_t(d_gate, phid[...])
        dup = dot_t(d_up, phid[...])
        gate_up = jnp.concatenate([dgp[:, 64:128], dup[:, 128:192]], axis=1)
        out = right[...] * weight
        ins = left[...]
        acc_out[...] = jnp.zeros(acc_out.shape, F32) if first else acc_in[...]
        me = me_ref[0]
        row = 0
        tn = (((0,), (0,)), ((), ()))
        for i, (offset, parts) in enumerate(sources):
            size = ROWS * sum(c for _, _, c in parts)
            mine = slice(row, row + size)
            row += size
            a = lax.dot_general(
                ins[mine, :64], gate_up[mine], tn, precision=lax.Precision.HIGHEST, preferred_element_type=F32
            )
            c = lax.dot_general(
                hid[mine, :64], out[mine], tn, precision=lax.Precision.HIGHEST, preferred_element_type=F32
            )
            turn[i, 0:64] = a
            turn[i, 64:128] = c
            even_a = turn[i, pl.ds(0, 32, stride=2)]
            odd_a = turn[i, pl.ds(1, 32, stride=2)]
            even_c = turn[i, pl.ds(64, 32, stride=2)]
            odd_c = turn[i, pl.ds(65, 32, stride=2)]
            total = jnp.concatenate(
                [
                    jnp.concatenate([even_a[:, :64], odd_a[:, :64]], axis=1),
                    jnp.concatenate([even_a[:, 64:], odd_a[:, 64:]], axis=1),
                    jnp.concatenate([even_c[:, 64:], odd_c[:, 64:]], axis=1),
                ],
                axis=0,
            )
            x_at = lax.rem(lax.rem(me, SIDE) - offset[0] + SIDE, SIDE)
            y_at = lax.rem(lax.div(me, SIDE) - offset[1] + SIDE, SIDE)
            acc_out[y_at * SIDE + x_at] += total


def step(blocks, me, weights, acc, acc_shape):
    wg, wu, wd, pin, phid = weights
    bufs, sources = [], []

    def index(buf):
        for i, other in enumerate(bufs):
            if other is buf:
                return i
        bufs.append(buf)
        return len(bufs) - 1

    for offset, parts in blocks.items():
        sources.append((offset, [(index(b), s, c) for b, s, c in parts]))
    n_rows = ROWS * sum(c for s in sources for _, _, c in s[1])
    ff = wg.shape[1]
    depth = wg.shape[2]
    full = lambda shape: pl.BlockSpec(shape, lambda k, s: (0,) * len(shape))
    in_specs = []
    for b in bufs:
        in_specs += [
            pl.BlockSpec((b.shape[0], ROWS, DEPTH), lambda k, s: (0, 0, k)),
            pl.BlockSpec((b.shape[0], ROWS, DEPTH), lambda k, s: (0, 0, k + depth // DEPTH)),
            pl.BlockSpec((b.shape[0], ROWS, LANES), lambda k, s: (0, 0, 2 * depth // LANES)),
        ]
    in_specs += [
        pl.BlockSpec((1, ff, DEPTH), lambda k, s: (0, 0, k)),
        pl.BlockSpec((1, ff, DEPTH), lambda k, s: (0, 0, k)),
        pl.BlockSpec((1, ff, DEPTH), lambda k, s: (0, 0, k)),
        pl.BlockSpec((DEPTH, 128), lambda k, s: (k, 0)),
        full(phid.shape),
    ]
    args = [me] + [b for b in bufs for _ in range(3)] + [wg, wu, wd, pin, phid]
    first = acc is None
    aliases = {}
    if not first:
        aliases = {len(args): 0}
        args.append(acc)
        in_specs.append(full(acc_shape))
    return pl.pallas_call(
        lambda *refs: step_kernel(sources, len(bufs), first, *refs),
        grid_spec=pltpu.PrefetchScalarGridSpec(
            num_scalar_prefetch=1,
            grid=(depth // DEPTH,),
            in_specs=in_specs,
            out_specs=full(acc_shape),
            scratch_shapes=[
                pltpu.VMEM((n_rows, ff), F32),
                pltpu.VMEM((n_rows, ff), F32),
                pltpu.VMEM((n_rows, ff), F32),
                pltpu.VMEM((n_rows, 128), F32),
                pltpu.VMEM((n_rows, 128), F32),
                pltpu.VMEM((len(sources), 128, 128), F32),
            ],
        ),
        out_shape=jax.ShapeDtypeStruct(acc_shape, F32),
        input_output_aliases=aliases,
        compiler_params=pltpu.CompilerParams(vmem_limit_bytes=32 * 1024 * 1024),
        cost_estimate=pl.CostEstimate(
            flops=2 * n_rows * depth * ff * 3, bytes_accessed=2 * depth * ff * 3, transcendentals=n_rows * ff
        ),
        name="expert_step",
    )(*args)


def shift(block, axis, way):
    moves = []
    for y in range(SIDE):
        for x in range(SIDE):
            to = (y, (x + way) % SIDE) if axis == 0 else ((y + way) % SIDE, x)
            moves.append((y * SIDE + x, to[0] * SIDE + to[1]))
    return lax.ppermute(block, "dp", moves)


def per_device(tokens, out_grads, routes, gate_codes, w_gate, w_up, w_down, proj_in, proj_hidden):
    n_dp = lax.axis_size("dp")
    n_exp = lax.axis_size("expert")
    cap = tokens.shape[0] // 4
    width = tokens.shape[1]
    rank = proj_in.shape[1] // 2
    me = lax.axis_index("dp").astype(jnp.int32).reshape(1)
    picks, codes = place_rows(routes, gate_codes, n_exp, cap, lax.axis_index("expert"))
    both = jnp.concatenate([tokens, out_grads], axis=1)
    slots = jnp.dot(picks, both, preferred_element_type=F32).astype(BF16)
    pieces = cap // ROWS
    slots = slots.reshape(n_exp, pieces, ROWS, 2, width)
    slots = lax.all_to_all(slots, "expert", split_axis=0, concat_axis=0, tiled=True)
    codes = codes.reshape(pieces, ROWS, 1)
    lane = jnp.arange(LANES, dtype=jnp.int32)
    meta = jnp.where(lane == 0, codes // 16, jnp.where(lane == 1, codes % 16, 0)).astype(BF16)
    own = slots.transpose(1, 2, 3, 0, 4).reshape(pieces, ROWS, 2 * n_exp * width)
    own = jnp.concatenate([own, meta], axis=2)

    weights = (w_gate.transpose(0, 2, 1), w_up.transpose(0, 2, 1), w_down, proj_in, proj_hidden.T)
    acc_shape = (n_dp, 3 * rank * rank // LANES, LANES)
    half = pieces // 2
    whole = lambda buf: [(buf, 0, pieces)]
    run = lambda blocks, acc: step(blocks, me, weights, acc, acc_shape)
    b10, b30, b01, b03 = shift(own, 0, 1), shift(own, 0, -1), shift(own, 1, 1), shift(own, 1, -1)
    b11, b33, b13, b31 = shift(b10, 1, 1), shift(b30, 1, -1), shift(b03, 0, 1), shift(b01, 0, -1)
    acc = run(
        {(0, 0): whole(own), (1, 0): whole(b10), (3, 0): whole(b30), (0, 1): whole(b01), (0, 3): whole(b03)}, None
    )
    b11, b33, b13, b31, acc = lax.optimization_barrier((b11, b33, b13, b31, acc))
    b21, b23, b12, b32 = shift(b11, 0, 1), shift(b33, 0, -1), shift(b13, 1, -1), shift(b31, 1, 1)
    acc = run({(1, 1): whole(b11), (3, 3): whole(b33), (1, 3): whole(b13), (3, 1): whole(b31)}, acc)
    b21, b23, b12, b32, acc = lax.optimization_barrier((b21, b23, b12, b32, acc))
    cat = lambda *parts: jnp.concatenate(parts, axis=0)
    east, west = shift(cat(b10[:half], b12[0:1]), 0, 1), shift(cat(b30[half:], b32[1:2]), 0, -1)
    north, south = shift(cat(b01[:half], b21[2:3]), 1, 1), shift(cat(b03[half:], b23[3:4]), 1, -1)
    acc = run({(2, 1): whole(b21), (2, 3): whole(b23), (1, 2): whole(b12), (3, 2): whole(b32)}, acc)
    acc = run(
        {
            (2, 0): [(east, 0, half), (west, 0, half)],
            (0, 2): [(north, 0, half), (south, 0, half)],
            (2, 2): [(q, half, 1) for q in (east, west, north, south)],
        },
        acc,
    )

    share = acc.reshape(n_dp, n_dp, -1, LANES).transpose(1, 2, 0, 3)
    share = lax.all_to_all(share, "dp", split_axis=0, concat_axis=0, tiled=True)
    total = jnp.sum(share, axis=0)
    return total.transpose(1, 0, 2).reshape(n_dp, 1, -1)


def solution(mesh):
    return jax.shard_map(
        per_device,
        mesh=mesh,
        in_specs=(
            P("dp", "expert"),
            P("dp", "expert"),
            P("dp", None),
            P("dp", None),
            P("expert", None, "dp"),
            P("expert", None, "dp"),
            P("expert", "dp", None),
            P(),
            P("dp", None),
        ),
        out_specs=P(None, "expert", "dp"),
        check_vma=False,
    )
```

profile of v0, /device:TPU:2, one launch (start us, length us, event | category | flops | bytes accessed | tf_op | source)
XLA Modules:
  0.0 181.9 jit_solution(15334791943554247481)
XLA Ops:
  0.0 0.8 copy.44
  1.5 0.7 multiply_add_fusion.1
  2.2 1.4 convolution_convert_fusion
  3.6 1.1 reshape.127
  4.7 8.7 %all-to-all-start = ((bf16[16,4,16,2,256]{4,3,2,1,0:T(2,128)(2,1)}), bf16[16,4,16,2,256]{4,3,2,1,0:T(2,128)(2,1)S(1)}, u32[]{:S(2)}, u32[]{:S(2)}) async-start(bf16[16,4,16,2,256]{4,3,2,1,0:T(2,128)(2,1)} %reshape.127), calls=%async_computation | async-start | bytes 2097152 | tf_op jit(solution)/shard_map/all_to_all | solution.py:206
  14.2 25.9 %all-to-all-done = bf16[16,4,16,2,256]{4,3,2,1,0:T(2,128)(2,1)S(1)} async-done(((bf16[16,4,16,2,256]{4,3,2,1,0:T(2,128)(2,1)}), bf16[16,4,16,2,256]{4,3,2,1,0:T(2,128)(2,1)S(1)}, u32[]{:S(2)}, u32[]{:S(2)}) %all-to-all-start) | async-done | bytes 1048608 | tf_op jit(solution)/shard_map/all_to_all | solution.py:206
  40.1 2.1 %copy.46 = bf16[4,16,2,16,256]{4,3,2,1,0:T(8,128)(2,1)} copy(bf16[4,16,2,16,256]{4,2,1,0,3:T(2,128)(2,1)S(1)} %bitcast.25) | data formatting | bytes 2097152 | tf_op jit(solution)/shard_map/transpose | solution.py:210
  42.2 2.5 %reshape.128 = bf16[4,16,8192]{2,1,0:T(8,128)(2,1)} reshape(bf16[4,16,2,16,256]{4,3,2,1,0:T(8,128)(2,1)} %copy.46) | data formatting | bytes 2097152 | tf_op jit(solution)/shard_map/reshape | solution.py:210
  44.7 1.3 pad_maximum_fusion.refs_1_.refs_2_.refs_3_
  46.1 1.6 collective-permute-start
  47.6 0.5 collective-permute-start.2
  48.2 3.0 %collective-permute-start.4 = (bf16[4,16,8320]{2,1,0:T(8,128)(2,1)S(1)}, bf16[4,16,8320]{2,1,0:T(8,128)(2,1)}, u32[]{:S(2)}, u32[]{:S(2)}) collective-permute-start(bf16[4,16,8320]{2,1,0:T(8,128)(2,1)S(1)} %pad_maximum_fusion.refs_1_.refs_2_.refs_3_), channel_id=1, source_target_pairs={{0,192},{16,208},{32,224},{48,240},{64,0},{80,16},{96,32},{112,48}... | collective-permute-start | bytes 3194888 | tf_op jit(solution)/shard_map/ppermute | solution.py:191
  51.2 1.0 copy-done.5
  52.2 19.7 %collective-permute-done.refs_4_.refs_5_.refs_6_ = bf16[4,16,8320]{2,1,0:T(8,128)(2,1)} collective-permute-done((bf16[4,16,8320]{2,1,0:T(8,128)(2,1)S(1)}, bf16[4,16,8320]{2,1,0:T(8,128)(2,1)}, u32[]{:S(2)}, u32[]{:S(2)}) %collective-permute-start) | collective-permute-done | bytes 1064992 | tf_op jit(solution)/shard_map/ppermute | solution.py:191
  72.0 1.6 collective-permute-start.1
  73.8 3.0 %collective-permute-start.3 = (bf16[4,16,8320]{2,1,0:T(8,128)(2,1)}, bf16[4,16,8320]{2,1,0:T(8,128)(2,1)}, u32[]{:S(2)}, u32[]{:S(2)}) collective-permute-start(bf16[4,16,8320]{2,1,0:T(8,128)(2,1)} %collective-permute-done.2.refs_7_.refs_8_.refs_9_), channel_id=1, source_target_pairs={{0,192},{16,208},{32,224},{48,240},{64,0},{80,16},{96,32},{112,48}... | collective-permute-start | bytes 3194888 | tf_op jit(solution)/shard_map/ppermute | solution.py:191
  76.8 1.2 collective-permute-start.5
  78.0 0.9 collective-permute-done.6.refs_10_.refs_11_.refs_12_
  78.9 1.7 collective-permute-start.7
  80.6 1.9 %copy-done.1 = bf16[1,4096,400]{1,2,0:T(8,128)(2,1)S(1)} copy-done((bf16[1,4096,400]{1,2,0:T(8,128)(2,1)S(1)}, bf16[1,4096,400]{1,2,0:T(8,128)(2,1)}, u32[]{:S(2)}) %copy-start.1) | copy-done | bytes 3276824
  82.6 1.9 %copy-done.3 = bf16[1,400,4096]{2,1,0:T(8,128)(2,1)S(1)} copy-done((bf16[1,400,4096]{2,1,0:T(8,128)(2,1)S(1)}, bf16[1,400,4096]{2,1,0:T(8,128)(2,1)}, u32[]{:S(2)}) %copy-start.3) | copy-done | bytes 3276824
  84.5 1.2 copy-done.6
  85.7 1.2 copy-done.7
  86.9 10.1 %expert_step.4.refs_18_ = f32[16,96,128]{2,1,0:T(8,128)S(1)} custom-call(s32[1]{0:T(128)} %bitcast.refs_0_, bf16[4,16,8320]{2,1,0:T(8,128)(2,1)S(1)} %copy-done.6, bf16[4,16,8320]{2,1,0:T(8,128)(2,1)S(1)} %copy-done.6, bf16[4,16,8320]{2,1,0:T(8,128)(2,1)S(1)} %copy-done.6, bf16[4,16,8320]{2,1,0:T(8,128)(2,1)} %collective-permute-done.refs_4_.refs_5_.refs_6_, ...), custom_call_target="tpu_custom_call" | custom-call | flops 3145728000 | bytes 9830400 | tf_op jit(solution)/shard_map/expert_step/pallas_call | solution.py:159
  97.0 4.5 %collective-permute-done.1.refs_1_.refs_2_.refs_3_ = bf16[4,16,8320]{2,1,0:T(8,128)(2,1)} collective-permute-done((bf16[4,16,8320]{2,1,0:T(8,128)(2,1)}, bf16[4,16,8320]{2,1,0:T(8,128)(2,1)}, u32[]{:S(2)}, u32[]{:S(2)}) %collective-permute-start.1) | collective-permute-done | bytes 1064992 | tf_op jit(solution)/shard_map/ppermute | solution.py:191
  101.6 1.1 collective-permute-done.5.refs_7_.refs_8_.refs_9_
  102.7 1.8 collective-permute-done.7.refs_10_.refs_11_.refs_12_
  104.5 1.3 collective-permute-start.10
  105.8 0.7 collective-permute-start.11
  106.5 1.5 collective-permute-start.8
  108.5 1.2 slice.45
  109.8 1.1 slice.44
  110.8 1.1 slice.43
  111.9 1.1 slice.42
  113.0 8.4 %expert_step.5.refs_18_ = f32[16,96,128]{2,1,0:T(8,128)S(1)} custom-call(s32[1]{0:T(128)} %bitcast.refs_0_, bf16[4,16,8320]{2,1,0:T(8,128)(2,1)} %collective-permute-done.1.refs_1_.refs_2_.refs_3_, bf16[4,16,8320]{2,1,0:T(8,128)(2,1)} %collective-permute-done.1.refs_1_.refs_2_.refs_3_, ...), custom_call_target="tpu_custom_call", output_to_operand_aliasing={{}: (18, {})} | custom-call | flops 2516582400 | bytes 9830400 | tf_op jit(solution)/shard_map/expert_step/pallas_call | solution.py:159
  121.5 7.6 %collective-permute-done.10.refs_7_.refs_8_.refs_9_ = bf16[4,16,8320]{2,1,0:T(8,128)(2,1)S(1)} collective-permute-done((bf16[4,16,8320]{2,1,0:T(8,128)(2,1)}, bf16[4,16,8320]{2,1,0:T(8,128)(2,1)S(1)}, u32[]{:S(2)}, u32[]{:S(2)}) %collective-permute-start.10) | collective-permute-done | bytes 1064992 | tf_op jit(solution)/shard_map/ppermute | solution.py:191
  129.1 2.2 %collective-permute-done.11.refs_10_.refs_11_.refs_12_ = bf16[4,16,8320]{2,1,0:T(8,128)(2,1)S(1)} collective-permute-done((bf16[4,16,8320]{2,1,0:T(8,128)(2,1)}, bf16[4,16,8320]{2,1,0:T(8,128)(2,1)S(1)}, u32[]{:S(2)}, u32[]{:S(2)}) %collective-permute-start.11) | collective-permute-done | bytes 1064992 | tf_op jit(solution)/shard_map/ppermute | solution.py:191
  131.3 1.1 collective-permute-done.9.refs_4_.refs_5_.refs_6_
  132.5 2.8 %collective-permute-start.15 = (bf16[3,16,8320]{2,1,0:T(8,128)(2,1)S(1)}, bf16[3,16,8320]{2,1,0:T(8,128)(2,1)S(1)}, u32[]{:S(2)}, u32[]{:S(2)}) collective-permute-start(bf16[3,16,8320]{2,1,0:T(8,128)(2,1)S(1)} %pad_maximum_fusion.4), channel_id=1, source_target_pairs={{0,192},{16,208},{32,224},{48,240},{64,0},{80,16},{96,32},{112,48}... | collective-permute-start | bytes 2396168 | tf_op jit(solution)/shard_map/ppermute | solution.py:191
  135.9 1.3 collective-permute-start.13
  137.3 0.9 collective-permute-start.12
  138.2 8.8 %expert_step.6.refs_18_ = f32[16,96,128]{2,1,0:T(8,128)S(1)} custom-call(s32[1]{0:T(128)} %bitcast.refs_0_, bf16[4,16,8320]{2,1,0:T(8,128)(2,1)S(1)} %collective-permute-done.8.refs_1_.refs_2_.refs_3_, bf16[4,16,8320]{2,1,0:T(8,128)(2,1)S(1)} %collective-permute-done.8.refs_1_.refs_2_.refs_3_, ...), custom_call_target="tpu_custom_call", output_to_operand_aliasing={{}: (18, {})} | custom-call | flops 2516582400 | bytes 9830400 | tf_op jit(solution)/shard_map/expert_step/pallas_call | solution.py:159
  147.0 3.0 %collective-permute-done.15.refs_10_.refs_11_.refs_12_ = bf16[3,16,8320]{2,1,0:T(8,128)(2,1)S(1)} collective-permute-done((bf16[3,16,8320]{2,1,0:T(8,128)(2,1)S(1)}, bf16[3,16,8320]{2,1,0:T(8,128)(2,1)S(1)}, u32[]{:S(2)}, u32[]{:S(2)}) %collective-permute-start.15) | collective-permute-done | bytes 798752 | tf_op jit(solution)/shard_map/ppermute | solution.py:191
  150.0 3.8 %collective-permute-done.14.refs_7_.refs_8_.refs_9_ = bf16[3,16,8320]{2,1,0:T(8,128)(2,1)S(1)} collective-permute-done((bf16[3,16,8320]{2,1,0:T(8,128)(2,1)S(1)}, bf16[3,16,8320]{2,1,0:T(8,128)(2,1)S(1)}, u32[]{:S(2)}, u32[]{:S(2)}) %collective-permute-start.14) | collective-permute-done | bytes 798752 | tf_op jit(solution)/shard_map/ppermute | solution.py:191
  153.9 1.4 collective-permute-done.12.refs_1_.refs_2_.refs_3_
  155.2 8.3 %expert_step.7 = f32[16,96,128]{2,1,0:T(8,128)S(1)} custom-call(s32[1]{0:T(128)} %bitcast.refs_0_, bf16[3,16,8320]{2,1,0:T(8,128)(2,1)S(1)} %collective-permute-done.12.refs_1_.refs_2_.refs_3_, bf16[3,16,8320]{2,1,0:T(8,128)(2,1)S(1)} %collective-permute-done.12.refs_1_.refs_2_.refs_3_, ...), custom_call_target="tpu_custom_call", output_to_operand_aliasing={{}: (18, {})} | custom-call | flops 1887436800 | bytes 9830400 | tf_op jit(solution)/shard_map/expert_step/pallas_call | solution.py:159
  164.0 17.1 %all_to_all.10 = f32[16,6,16,128]{3,2,1,0:T(8,128)S(1)} all-to-all(f32[16,6,16,128]{3,2,1,0:T(8,128)S(1)} %bitcast.26), channel_id=1, replica_groups=mesh['dp'=16,'expert'=16] {'dp'}, dimensions={0} | all-to-all | bytes 1572864 | tf_op jit(solution)/shard_map/all_to_all | solution.py:241
  181.2 0.7 reshape.132
  (51 shorter events, 3.4 us)
Async XLA Ops:
  4.7 8.7 %copy-start.10 = (s32[256,2]{0,1:T(2,128)S(1)}, s32[256,2]{0,1:T(2,128)}, u32[]{:S(2)}) copy-start(s32[256,2]{0,1:T(2,128)} %param.12) | copy-start | bytes 6148
  4.7 35.4 %all-to-all-start = ((bf16[16,4,16,2,256]{4,3,2,1,0:T(2,128)(2,1)}), bf16[16,4,16,2,256]{4,3,2,1,0:T(2,128)(2,1)S(1)}, u32[]{:S(2)}, u32[]{:S(2)}) async-start(bf16[16,4,16,2,256]{4,3,2,1,0:T(2,128)(2,1)} %reshape.127), calls=%async_computation | async-start | bytes 2097152 | tf_op jit(solution)/shard_map/all_to_all | solution.py:206
  42.2 38.4 %copy-start = (bf16[1,4096,400]{1,2,0:T(8,128)(2,1)S(1)}, bf16[1,4096,400]{1,2,0:T(8,128)(2,1)}, u32[]{:S(2)}) copy-start(bf16[1,4096,400]{1,2,0:T(8,128)(2,1)} %param.13) | copy-start | bytes 9830404
  44.7 35.9 %copy-start.9 = (bf16[400,192]{0,1:T(8,128)(2,1)S(1)}, bf16[400,192]{0,1:T(8,128)(2,1)}, u32[]{:S(2)}) copy-start(bf16[400,192]{0,1:T(8,128)(2,1)} %param.17) | copy-start | bytes 460804
  46.1 25.9 %collective-permute-start = (bf16[4,16,8320]{2,1,0:T(8,128)(2,1)S(1)}, bf16[4,16,8320]{2,1,0:T(8,128)(2,1)}, u32[]{:S(2)}, u32[]{:S(2)}) collective-permute-start(bf16[4,16,8320]{2,1,0:T(8,128)(2,1)S(1)} %pad_maximum_fusion.refs_1_.refs_2_.refs_3_), channel_id=1, source_target_pairs={{0,16},{16,32},{32,48},{48,0},{64,80},{80,96},{96,112},{112,64},{1... | collective-permute-start | bytes 3194888 | tf_op jit(solution)/shard_map/ppermute | solution.py:191
  47.6 26.1 %collective-permute-start.2 = (bf16[4,16,8320]{2,1,0:T(8,128)(2,1)S(1)}, bf16[4,16,8320]{2,1,0:T(8,128)(2,1)}, u32[]{:S(2)}, u32[]{:S(2)}) collective-permute-start(bf16[4,16,8320]{2,1,0:T(8,128)(2,1)S(1)} %pad_maximum_fusion.refs_1_.refs_2_.refs_3_), channel_id=1, source_target_pairs={{0,48},{16,0},{32,16},{48,32},{64,112},{80,64},{96,80},{112,96},{1... | collective-permute-start | bytes 3194888 | tf_op jit(solution)/shard_map/ppermute | solution.py:191
  48.2 28.6 %collective-permute-start.4 = (bf16[4,16,8320]{2,1,0:T(8,128)(2,1)S(1)}, bf16[4,16,8320]{2,1,0:T(8,128)(2,1)}, u32[]{:S(2)}, u32[]{:S(2)}) collective-permute-start(bf16[4,16,8320]{2,1,0:T(8,128)(2,1)S(1)} %pad_maximum_fusion.refs_1_.refs_2_.refs_3_), channel_id=1, source_target_pairs={{0,192},{16,208},{32,224},{48,240},{64,0},{80,16},{96,32},{112,48}... | collective-permute-start | bytes 3194888 | tf_op jit(solution)/shard_map/ppermute | solution.py:191
  51.2 27.7 %collective-permute-start.6 = (bf16[4,16,8320]{2,1,0:T(8,128)(2,1)S(1)}, bf16[4,16,8320]{2,1,0:T(8,128)(2,1)}, u32[]{:S(2)}, u32[]{:S(2)}) collective-permute-start(bf16[4,16,8320]{2,1,0:T(8,128)(2,1)S(1)} %pad_maximum_fusion.refs_1_.refs_2_.refs_3_), channel_id=1, source_target_pairs={{0,64},{16,80},{32,96},{48,112},{64,128},{80,144},{96,160},{112,17... | collective-permute-start | bytes 3194888 | tf_op jit(solution)/shard_map/ppermute | solution.py:191
  51.2 1.0 copy-start.5
  72.0 29.6 %collective-permute-start.1 = (bf16[4,16,8320]{2,1,0:T(8,128)(2,1)}, bf16[4,16,8320]{2,1,0:T(8,128)(2,1)}, u32[]{:S(2)}, u32[]{:S(2)}) collective-permute-start(bf16[4,16,8320]{2,1,0:T(8,128)(2,1)} %collective-permute-done.refs_4_.refs_5_.refs_6_), channel_id=1, source_target_pairs={{0,64},{16,80},{32,96},{48,112},{64,128},{80,144},{96,160},{112,17... | collective-permute-start | bytes 3194888 | tf_op jit(solution)/shard_map/ppermute | solution.py:191
  73.8 27.8 %collective-permute-start.3 = (bf16[4,16,8320]{2,1,0:T(8,128)(2,1)}, bf16[4,16,8320]{2,1,0:T(8,128)(2,1)}, u32[]{:S(2)}, u32[]{:S(2)}) collective-permute-start(bf16[4,16,8320]{2,1,0:T(8,128)(2,1)} %collective-permute-done.2.refs_7_.refs_8_.refs_9_), channel_id=1, source_target_pairs={{0,192},{16,208},{32,224},{48,240},{64,0},{80,16},{96,32},{112,48}... | collective-permute-start | bytes 3194888 | tf_op jit(solution)/shard_map/ppermute | solution.py:191
  76.8 25.9 %collective-permute-start.5 = (bf16[4,16,8320]{2,1,0:T(8,128)(2,1)}, bf16[4,16,8320]{2,1,0:T(8,128)(2,1)}, u32[]{:S(2)}, u32[]{:S(2)}) collective-permute-start(bf16[4,16,8320]{2,1,0:T(8,128)(2,1)} %collective-permute-done.4.refs_13_.refs_14_.refs_15_), channel_id=1, source_target_pairs={{0,16},{16,32},{32,48},{48,0},{64,80},{80,96},{96,112},{112,64},{1... | collective-permute-start | bytes 3194888 | tf_op jit(solution)/shard_map/ppermute | solution.py:191
  78.9 25.6 %collective-permute-start.7 = (bf16[4,16,8320]{2,1,0:T(8,128)(2,1)}, bf16[4,16,8320]{2,1,0:T(8,128)(2,1)}, u32[]{:S(2)}, u32[]{:S(2)}) collective-permute-start(bf16[4,16,8320]{2,1,0:T(8,128)(2,1)} %collective-permute-done.6.refs_10_.refs_11_.refs_12_), channel_id=1, source_target_pairs={{0,48},{16,0},{32,16},{48,32},{64,112},{80,64},{96,80},{112,96},{1... | collective-permute-start | bytes 3194888 | tf_op jit(solution)/shard_map/ppermute | solution.py:191
  80.6 1.9 %copy-start.1 = (bf16[1,4096,400]{1,2,0:T(8,128)(2,1)S(1)}, bf16[1,4096,400]{1,2,0:T(8,128)(2,1)}, u32[]{:S(2)}) copy-start(bf16[1,4096,400]{1,2,0:T(8,128)(2,1)} %param.14) | copy-start | bytes 9830404
  82.6 1.9 %copy-start.3 = (bf16[1,400,4096]{2,1,0:T(8,128)(2,1)S(1)}, bf16[1,400,4096]{2,1,0:T(8,128)(2,1)}, u32[]{:S(2)}) copy-start(bf16[1,400,4096]{2,1,0:T(8,128)(2,1)} %refs_15_.5) | copy-start | bytes 9830404
  84.5 1.2 copy-start.6
  85.7 1.2 copy-start.7
  86.9 26.1 %copy-start.4 = (bf16[1,400,4096]{2,1,0:T(8,128)(2,1)S(1)}, bf16[1,400,4096]{2,1,0:T(8,128)(2,1)}, u32[]{:S(2)}) copy-start(bf16[1,400,4096]{2,1,0:T(8,128)(2,1)} %refs_15_.5) | copy-start | bytes 9830404
  86.9 26.1 %copy-start.8 = (bf16[4096,128]{1,0:T(8,128)(2,1)S(1)}, bf16[4096,128]{1,0:T(8,128)(2,1)}, u32[]{:S(2)}) copy-start(bf16[4096,128]{1,0:T(8,128)(2,1)} %refs_16_.5) | copy-start | bytes 3145732
  104.5 24.6 %collective-permute-start.10 = (bf16[4,16,8320]{2,1,0:T(8,128)(2,1)}, bf16[4,16,8320]{2,1,0:T(8,128)(2,1)S(1)}, u32[]{:S(2)}, u32[]{:S(2)}) collective-permute-start(bf16[4,16,8320]{2,1,0:T(8,128)(2,1)} %collective-permute-done.5.refs_7_.refs_8_.refs_9_), channel_id=1, source_target_pairs={{0,192},{16,208},{32,224},{48,240},{64,0},{80,16},{96,32},{112,48}... | collective-permute-start | bytes 3194888 | tf_op jit(solution)/shard_map/ppermute | solution.py:191
  105.8 25.5 %collective-permute-start.11 = (bf16[4,16,8320]{2,1,0:T(8,128)(2,1)}, bf16[4,16,8320]{2,1,0:T(8,128)(2,1)S(1)}, u32[]{:S(2)}, u32[]{:S(2)}) collective-permute-start(bf16[4,16,8320]{2,1,0:T(8,128)(2,1)} %collective-permute-done.7.refs_10_.refs_11_.refs_12_), channel_id=1, source_target_pairs={{0,64},{16,80},{32,96},{48,112},{64,128},{80,144},{96,160},{112,17... | collective-permute-start | bytes 3194888 | tf_op jit(solution)/shard_map/ppermute | solution.py:191
  106.5 24.8 %collective-permute-start.8 = (bf16[4,16,8320]{2,1,0:T(8,128)(2,1)}, bf16[4,16,8320]{2,1,0:T(8,128)(2,1)S(1)}, u32[]{:S(2)}, u32[]{:S(2)}) collective-permute-start(bf16[4,16,8320]{2,1,0:T(8,128)(2,1)} %collective-permute-done.1.refs_1_.refs_2_.refs_3_), channel_id=1, source_target_pairs={{0,16},{16,32},{32,48},{48,0},{64,80},{80,96},{96,112},{112,64},{1... | collective-permute-start | bytes 3194888 | tf_op jit(solution)/shard_map/ppermute | solution.py:191
  108.0 24.4 %collective-permute-start.9 = (bf16[4,16,8320]{2,1,0:T(8,128)(2,1)}, bf16[4,16,8320]{2,1,0:T(8,128)(2,1)S(1)}, u32[]{:S(2)}, u32[]{:S(2)}) collective-permute-start(bf16[4,16,8320]{2,1,0:T(8,128)(2,1)} %collective-permute-done.3.refs_4_.refs_5_.refs_6_), channel_id=1, source_target_pairs={{0,48},{16,0},{32,16},{48,32},{64,112},{80,64},{96,80},{112,96},{1... | collective-permute-start | bytes 3194888 | tf_op jit(solution)/shard_map/ppermute | solution.py:191
  108.5 4.5 %copy-start.2 = (bf16[1,4096,400]{1,2,0:T(8,128)(2,1)S(1)}, bf16[1,4096,400]{1,2,0:T(8,128)(2,1)}, u32[]{:S(2)}) copy-start(bf16[1,4096,400]{1,2,0:T(8,128)(2,1)} %param.14) | copy-start | bytes 9830404
  132.5 17.5 %collective-permute-start.15 = (bf16[3,16,8320]{2,1,0:T(8,128)(2,1)S(1)}, bf16[3,16,8320]{2,1,0:T(8,128)(2,1)S(1)}, u32[]{:S(2)}, u32[]{:S(2)}) collective-permute-start(bf16[3,16,8320]{2,1,0:T(8,128)(2,1)S(1)} %pad_maximum_fusion.4), channel_id=1, source_target_pairs={{0,192},{16,208},{32,224},{48,240},{64,0},{80,16},{96,32},{112,48}... | collective-permute-start | bytes 2396168 | tf_op jit(solution)/shard_map/ppermute | solution.py:191
  135.4 18.4 %collective-permute-start.14 = (bf16[3,16,8320]{2,1,0:T(8,128)(2,1)S(1)}, bf16[3,16,8320]{2,1,0:T(8,128)(2,1)S(1)}, u32[]{:S(2)}, u32[]{:S(2)}) collective-permute-start(bf16[3,16,8320]{2,1,0:T(8,128)(2,1)S(1)} %pad_maximum_fusion.3), channel_id=1, source_target_pairs={{0,64},{16,80},{32,96},{48,112},{64,128},{80,144},{96,160},{112,17... | collective-permute-start | bytes 2396168 | tf_op jit(solution)/shard_map/ppermute | solution.py:191
  135.9 18.0 %collective-permute-start.13 = (bf16[3,16,8320]{2,1,0:T(8,128)(2,1)S(1)}, bf16[3,16,8320]{2,1,0:T(8,128)(2,1)S(1)}, u32[]{:S(2)}, u32[]{:S(2)}) collective-permute-start(bf16[3,16,8320]{2,1,0:T(8,128)(2,1)S(1)} %pad_maximum_fusion.2), channel_id=1, source_target_pairs={{0,48},{16,0},{32,16},{48,32},{64,112},{80,64},{96,80},{112,96},{1... | collective-permute-start | bytes 2396168 | tf_op jit(solution)/shard_map/ppermute | solution.py:191
  137.3 18.0 %collective-permute-start.12 = (bf16[3,16,8320]{2,1,0:T(8,128)(2,1)S(1)}, bf16[3,16,8320]{2,1,0:T(8,128)(2,1)S(1)}, u32[]{:S(2)}, u32[]{:S(2)}) collective-permute-start(bf16[3,16,8320]{2,1,0:T(8,128)(2,1)S(1)} %pad_maximum_fusion.1), channel_id=1, source_target_pairs={{0,16},{16,32},{32,48},{48,0},{64,80},{80,96},{96,112},{112,64},{1... | collective-permute-start | bytes 2396168 | tf_op jit(solution)/shard_map/ppermute | solution.py:191
where the time goes:
time: 182 us
  waiting for transfers between devices  73.4 us (40%)
  Pallas kernels  35.6 us (20%)
  starting transfers between devices  30.7 us (17%)
  local copies, waits for them, and re-layouts  20.3 us (11%)
  blocking collectives  17.1 us (9%)
  other arithmetic  2.73 us (2%)
    ppermute x16, waiting for transfers between devices, shift(): return lax.ppermute(block, 'dp', moves)  47.5 us
    pallas_call x4, Pallas kernels, step(): pl.pallas_call(lambda *refs: step_kernel(sources, len(bufs), first, *refs...  35.6 us
    all_to_all x1, waiting for transfers between devices, per_device(): lax.all_to_all(slots, 'expert', split_axis=0, concat_axis=0, tiled=True)  25.9 us
    ppermute x16, starting transfers between devices, shift(): return lax.ppermute(block, 'dp', moves)  22 us
    all_to_all x1, blocking collectives, per_device(): share = lax.all_to_all(share, 'dp', split_axis=0, concat_axis=0, tiled=True)  17.1 us
    all_to_all x1, starting transfers between devices, per_device(): lax.all_to_all(slots, 'expert', split_axis=0, concat_axis=0, tiled=True)  8.7 us
    unnamed x24, local copies, waits for them, and re-layouts  8.3 us
  transfers between devices with their start and end apart: 17, of which 13 were waited for; matrix products, arithmetic and copies ran while one was open for 3% of the time, Pallas kernels for 15%

commit v1 on v0

v1 whole, which is shorter than its diff:
```python
import jax
import jax.numpy as jnp
from jax import lax
from jax.experimental import pallas as pl
from jax.experimental.pallas import tpu as pltpu
from jax.sharding import PartitionSpec as P

SIDE = 4
ROWS = 16
LANES = 128
DEPTH = 1024
F32 = jnp.float32
BF16 = jnp.bfloat16


def pack_kernel(cap, mine_ref, routes_ref, codes_ref, tokens_ref, grads_ref, slots_ref, meta_ref):
    n_exp = slots_ref.shape[0]
    count = tokens_ref.shape[0]
    shape = (n_exp, count)
    expert = lax.broadcasted_iota(jnp.int32, shape, 0)
    hits = jnp.where(routes_ref[0:1] == expert, 1.0, 0.0) + jnp.where(routes_ref[1:2] == expert, 1.0, 0.0)
    earlier = lax.broadcasted_iota(jnp.int32, (count, count), 0) < lax.broadcasted_iota(jnp.int32, (count, count), 1)
    before = jnp.dot(hits.astype(BF16), jnp.where(earlier, 1.0, 0.0).astype(BF16), preferred_element_type=F32)
    place = jnp.where(hits > 0.0, before, -1.0)
    slot = lax.broadcasted_iota(jnp.int32, (cap, count), 0).astype(F32)
    values = jnp.concatenate([tokens_ref[...], grads_ref[...]], axis=1)
    width = tokens_ref.shape[1]
    for e in range(n_exp):
        picks = jnp.where(place[e : e + 1] == slot, 1.0, 0.0).astype(BF16)
        rows = jnp.dot(picks, values, preferred_element_type=F32).astype(BF16)
        slots_ref[e, 0] = rows[:, :width].reshape(cap // ROWS, ROWS, width)
        slots_ref[e, 1] = rows[:, width:].reshape(cap // ROWS, ROWS, width)
    mine = mine_ref[0]
    here = jnp.sum(jnp.where(expert == mine, place, 0.0), axis=0, keepdims=True)
    named = jnp.where(routes_ref[0:1] == mine, codes_ref[0:1], 0) + jnp.where(
        routes_ref[1:2] == mine, codes_ref[1:2], 0
    )
    codes = jnp.sum(jnp.where(here == slot, named, 0).astype(F32), axis=1, keepdims=True)
    high = jnp.floor(codes * (1.0 / 16.0))
    lane = lax.broadcasted_iota(jnp.int32, (cap, LANES), 1)
    meta = jnp.where(lane == 0, high, jnp.where(lane == 1, codes - 16.0 * high, 0.0))
    meta_ref[...] = meta.astype(BF16).reshape(cap // ROWS, ROWS, LANES)


def lay_kernel(slots_ref, meta_ref, own_ref):
    n_exp, sides, _, _, width = slots_ref.shape
    for w in range(sides):
        for d in range(n_exp):
            at = (w * n_exp + d) * width
            own_ref[:, :, at : at + width] = slots_ref[d, w]
    own_ref[:, :, sides * n_exp * width :] = meta_ref[...]


def dot_t(rows, columns):
    return lax.dot_general(rows, columns, (((1,), (1,)), ((), ())), preferred_element_type=F32)


def step_kernel(sources, n_bufs, first, me_ref, *refs):
    bufs = refs[:n_bufs]
    wg, wu, wd, pin, phid = refs[n_bufs : n_bufs + 5]
    rest = refs[n_bufs + 5 :]
    acc_in = None if first else rest[0]
    acc_out, gate, upper, back, left, right, turn = rest[0 if first else 1 :]
    depth = wg.shape[2]

    def side(start, size):
        parts = [bufs[i][s : s + c, :, start : start + size] for _, parts in sources for i, s, c in parts]
        return jnp.concatenate([p.reshape(p.shape[0] * ROWS, size) for p in parts], axis=0)

    for at in range(0, depth, DEPTH):
        part = slice(at, at + DEPTH)
        xs = side(at, DEPTH)
        dys = side(depth + at, DEPTH)
        for ref, term in (
            (gate, dot_t(xs, wg[0, :, part])),
            (upper, dot_t(xs, wu[0, :, part])),
            (back, dot_t(dys, wd[0, :, part])),
            (left, jnp.dot(xs, pin[part], preferred_element_type=F32)),
            (right, jnp.dot(dys, pin[part], preferred_element_type=F32)),
        ):
            ref[...] = term if at == 0 else ref[...] + term

    codes = side(2 * depth, LANES).astype(F32)
    weight = (codes[:, 0:1] * 16.0 + codes[:, 1:2]) / 4096.0
    g = gate[...]
    u = upper[...]
    sig = jax.nn.sigmoid(g)
    act = g * sig
    hidden = (act * u).astype(BF16)
    b = back[...] * weight
    d_up = (b * act).astype(BF16)
    d_gate = (b * u * sig * (1.0 + g * (1.0 - sig))).astype(BF16)
    hid = dot_t(hidden, phid[...])
    dgp = dot_t(d_gate, phid[...])
    dup = dot_t(d_up, phid[...])
    gate_up = jnp.concatenate([dgp[:, 64:128], dup[:, 128:192]], axis=1)
    out = right[...] * weight
    ins = left[...]
    acc_out[...] = jnp.zeros(acc_out.shape, F32) if first else acc_in[...]
    me = me_ref[0]
    row = 0
    tn = (((0,), (0,)), ((), ()))
    for i, (offset, parts) in enumerate(sources):
        size = ROWS * sum(c for _, _, c in parts)
        mine = slice(row, row + size)
        row += size
        a = lax.dot_general(
            ins[mine, :64], gate_up[mine], tn, precision=lax.Precision.HIGHEST, preferred_element_type=F32
        )
        c = lax.dot_general(
            hid[mine, :64], out[mine], tn, precision=lax.Precision.HIGHEST, preferred_element_type=F32
        )
        turn[i, 0:64] = a
        turn[i, 64:128] = c
        even_a = turn[i, pl.ds(0, 32, stride=2)]
        odd_a = turn[i, pl.ds(1, 32, stride=2)]
        even_c = turn[i, pl.ds(64, 32, stride=2)]
        odd_c = turn[i, pl.ds(65, 32, stride=2)]
        total = jnp.concatenate(
            [
                jnp.concatenate([even_a[:, :64], odd_a[:, :64]], axis=1),
                jnp.concatenate([even_a[:, 64:], odd_a[:, 64:]], axis=1),
                jnp.concatenate([even_c[:, 64:], odd_c[:, 64:]], axis=1),
            ],
            axis=0,
        )
        x_at = lax.rem(lax.rem(me, SIDE) - offset[0] + SIDE, SIDE)
        y_at = lax.rem(lax.div(me, SIDE) - offset[1] + SIDE, SIDE)
        acc_out[y_at * SIDE + x_at] += total


def step(blocks, me, weights, acc, acc_shape):
    wg, wu, wd, pin, phid = weights
    bufs, sources = [], []

    def index(buf):
        for i, other in enumerate(bufs):
            if other is buf:
                return i
        bufs.append(buf)
        return len(bufs) - 1

    for offset, parts in blocks.items():
        sources.append((offset, [(index(b), s, c) for b, s, c in parts]))
    n_rows = ROWS * sum(c for s in sources for _, _, c in s[1])
    ff = wg.shape[1]
    depth = wg.shape[2]
    args = [me, *bufs, wg, wu, wd, pin, phid]
    first = acc is None
    aliases = {}
    if not first:
        aliases = {len(args): 0}
        args.append(acc)
    return pl.pallas_call(
        lambda *refs: step_kernel(sources, len(bufs), first, *refs),
        in_specs=[pl.BlockSpec(memory_space=pltpu.SMEM)] + [pl.BlockSpec(memory_space=pltpu.VMEM)] * (len(args) - 1),
        out_specs=pl.BlockSpec(memory_space=pltpu.VMEM),
        scratch_shapes=[
            pltpu.VMEM((n_rows, ff), F32),
            pltpu.VMEM((n_rows, ff), F32),
            pltpu.VMEM((n_rows, ff), F32),
            pltpu.VMEM((n_rows, 128), F32),
            pltpu.VMEM((n_rows, 128), F32),
            pltpu.VMEM((len(sources), 128, 128), F32),
        ],
        out_shape=jax.ShapeDtypeStruct(acc_shape, F32),
        input_output_aliases=aliases,
        compiler_params=pltpu.CompilerParams(vmem_limit_bytes=32 * 1024 * 1024),
        cost_estimate=pl.CostEstimate(
            flops=2 * n_rows * depth * ff * 3, bytes_accessed=2 * depth * ff * 3, transcendentals=n_rows * ff
        ),
        name="expert_step",
    )(*args)


def shift(block, axis, way):
    moves = []
    for y in range(SIDE):
        for x in range(SIDE):
            to = (y, (x + way) % SIDE) if axis == 0 else ((y + way) % SIDE, x)
            moves.append((y * SIDE + x, to[0] * SIDE + to[1]))
    return lax.ppermute(block, "dp", moves)


def after(acc, *bufs):
    held = []
    for buf in bufs:
        buf, acc = lax.optimization_barrier((buf, acc))
        held.append(buf)
    return (*held, acc)


def per_device(tokens, out_grads, routes, gate_codes, w_gate, w_up, w_down, proj_in, proj_hidden):
    n_dp = lax.axis_size("dp")
    n_exp = lax.axis_size("expert")
    cap = tokens.shape[0] // 4
    width = tokens.shape[1]
    rank = proj_in.shape[1] // 2
    me = lax.axis_index("dp").astype(jnp.int32).reshape(1)
    mine = lax.axis_index("expert").astype(jnp.int32).reshape(1)
    pieces = cap // ROWS
    vmem = pl.BlockSpec(memory_space=pltpu.VMEM)
    slots, meta = pl.pallas_call(
        lambda *refs: pack_kernel(cap, *refs),
        in_specs=[pl.BlockSpec(memory_space=pltpu.SMEM), vmem, vmem, vmem, vmem],
        out_specs=[vmem, vmem],
        out_shape=[
            jax.ShapeDtypeStruct((n_exp, 2, pieces, ROWS, width), BF16),
            jax.ShapeDtypeStruct((pieces, ROWS, LANES), BF16),
        ],
        name="pack_slots",
    )(mine, routes.T, gate_codes.T, tokens, out_grads)
    slots = lax.all_to_all(slots, "expert", split_axis=0, concat_axis=0, tiled=True)
    own = pl.pallas_call(
        lay_kernel,
        in_specs=[vmem, vmem],
        out_specs=vmem,
        out_shape=jax.ShapeDtypeStruct((pieces, ROWS, 2 * n_exp * width + LANES), BF16),
        name="lay_rows",
    )(slots, meta)

    weights = (w_gate.transpose(0, 2, 1), w_up.transpose(0, 2, 1), w_down, proj_in, proj_hidden.T)
    acc_shape = (n_dp, 3 * rank * rank // LANES, LANES)
    half = pieces // 2
    whole = lambda buf: [(buf, 0, pieces)]
    run = lambda blocks, acc: step(blocks, me, weights, acc, acc_shape)
    b10, b30, b01, b03 = shift(own, 0, 1), shift(own, 0, -1), shift(own, 1, 1), shift(own, 1, -1)
    b11, b33, b13, b31 = shift(b10, 1, 1), shift(b30, 1, -1), shift(b03, 0, 1), shift(b01, 0, -1)
    acc = run(
        {(0, 0): whole(own), (1, 0): whole(b10), (3, 0): whole(b30), (0, 1): whole(b01), (0, 3): whole(b03)}, None
    )
    b11, b33, b13, b31, acc = after(acc, b11, b33, b13, b31)
    b21, b23, b12, b32 = shift(b11, 0, 1), shift(b33, 0, -1), shift(b13, 1, -1), shift(b31, 1, 1)
    acc = run({(1, 1): whole(b11), (3, 3): whole(b33), (1, 3): whole(b13), (3, 1): whole(b31)}, acc)
    b21, b23, b12, b32, acc = after(acc, b21, b23, b12, b32)
    cat = lambda *parts: jnp.concatenate(parts, axis=0)
    east, west = shift(cat(b10[:half], b12[0:1]), 0, 1), shift(cat(b30[half:], b32[1:2]), 0, -1)
    north, south = shift(cat(b01[:half], b21[2:3]), 1, 1), shift(cat(b03[half:], b23[3:4]), 1, -1)
    acc = run({(2, 1): whole(b21), (2, 3): whole(b23), (1, 2): whole(b12), (3, 2): whole(b32)}, acc)
    acc = run(
        {
            (2, 0): [(east, 0, half), (west, 0, half)],
            (0, 2): [(north, 0, half), (south, 0, half)],
            (2, 2): [(q, half, 1) for q in (east, west, north, south)],
        },
        acc,
    )

    share = acc.reshape(n_dp, n_dp, -1, LANES).transpose(1, 2, 0, 3)
    share = lax.all_to_all(share, "dp", split_axis=0, concat_axis=0, tiled=True)
    total = jnp.sum(share, axis=0)
    return total.transpose(1, 0, 2).reshape(n_dp, 1, -1)


def solution(mesh):
    return jax.shard_map(
        per_device,
        mesh=mesh,
        in_specs=(
            P("dp", "expert"),
            P("dp", "expert"),
            P("dp", None),
            P("dp", None),
            P("expert", None, "dp"),
            P("expert", None, "dp"),
            P("expert", "dp", None),
            P(),
            P("dp", None),
        ),
        out_specs=P(None, "expert", "dp"),
        check_vma=False,
    )
```

time: 182 us -> 172 us (0.945)
  blocking collectives: 17.1 us -> 52.2 us
  waiting for transfers between devices: 73.4 us -> 51.1 us
  local copies, waits for them, and re-layouts: 20.3 us -> 12 us
  starting transfers between devices: 30.7 us -> 23.1 us
  Pallas kernels: 35.6 us -> 32.4 us
  other arithmetic: 2.73 us -> 0.41 us
    all_to_all x0 -> x1, blocking collectives: none -> 36.2 us  [per_device(): lax.all_to_all(slots, 'expert', split_axis=0, concat_axis=0, tiled=True)]
    all_to_all x1 -> x0, waiting for transfers between devices: 25.9 us -> none  [per_device(): lax.all_to_all(slots, 'expert', split_axis=0, concat_axis=0, tiled=True)]
    all_to_all x1 -> x0, starting transfers between devices: 8.7 us -> none  [per_device(): lax.all_to_all(slots, 'expert', split_axis=0, concat_axis=0, tiled=True)]
    pallas_call x4, Pallas kernels: 35.6 us -> 27.1 us  [step(): pl.pallas_call(lambda *refs: step_kernel(sources, len(bufs), first, *refs...]
    pallas_call x0 -> x2, Pallas kernels: none -> 5.31 us  [the longest x1 3 us: per_device(): pl.pallas_call(lambda *refs: pack_kernel(cap, *refs), in_specs=[pl.BlockS...]
    reshape x3 -> x0, local copies, waits for them, and re-layouts: 3.72 us -> none  [the longest x1 2.49 us: per_device(): slots.transpose(1, 2, 3, 0, 4).reshape(pieces, ROWS, 2 * n_exp * width)]
    ppermute x16, waiting for transfers between devices: 47.5 us -> 51.1 us  [shift(): return lax.ppermute(block, 'dp', moves)]
    transpose x1 -> x0, local copies, waits for them, and re-layouts: 2.12 us -> none  [per_device(): slots.transpose(1, 2, 3, 0, 4).reshape(pieces, ROWS, 2 * n_exp * width)]
  transfers between devices with their start and end apart: 17 -> 16, of which waited for: 13 -> 12; matrix products, arithmetic and copies ran while one was open for 3% -> 3% of each run, Pallas kernels for 15% -> 13%
where the time goes in v1:
time: 172 us; the launch traced here: 171 us
  blocking collectives  52.2 us (30%)
  waiting for transfers between devices  51.1 us (30%)
  Pallas kernels  32.4 us (19%)
  starting transfers between devices  23.1 us (13%)
  local copies, waits for them, and re-layouts  12 us (7%)
    ppermute x16, waiting for transfers between devices, shift(): return lax.ppermute(block, 'dp', moves)  51.1 us
    all_to_all x1, blocking collectives, per_device(): lax.all_to_all(slots, 'expert', split_axis=0, concat_axis=0, tiled=True)  36.2 us
    pallas_call x4, Pallas kernels, step(): pl.pallas_call(lambda *refs: step_kernel(sources, len(bufs), first, *refs...  27.1 us
    ppermute x16, starting transfers between devices, shift(): return lax.ppermute(block, 'dp', moves)  23.1 us
    all_to_all x1, blocking collectives, per_device(): share = lax.all_to_all(share, 'dp', split_axis=0, concat_axis=0, tiled=True)  16 us
    unnamed x18, local copies, waits for them, and re-layouts  6.33 us
  transfers between devices with their start and end apart: 16, of which 12 were waited for; matrix products, arithmetic and copies ran while one was open for 3% of the time, Pallas kernels for 13%

profile of v1, /device:TPU:2, one launch (start us, length us, event | category | flops | bytes accessed | tf_op | source)
XLA Modules:
  0.0 171.3 jit_solution(13708741662501142004)
XLA Ops:
  0.0 3.0 %pack_slots.1 = (bf16[16,2,4,16,256]{4,3,2,1,0:T(8,128)(2,1)}, bf16[4,16,128]{2,1,0:T(8,128)(2,1)}) custom-call(s32[1]{0:T(128)} %bitcast.1.refs_0_, s32[2,256]{1,0:T(2,128)} %bitcast.25, s32[2,256]{1,0:T(2,128)} %bitcast.26, bf16[256,256]{1,0:T(8,128)(2,1)} %refs_3_.1, bf16[256,256]{1,0:T(8,128)(2,1)} %refs_4_.1), custom_call_target="tpu_custom_call" | custom-call | tf_op jit(solution)/shard_map/pack_slots/pallas_call | solution.py:203
  3.0 36.2 %all_to_all.10.slots_ref = bf16[16,2,4,16,256]{4,3,2,1,0:T(8,128)(2,1)} all-to-all(bf16[16,2,4,16,256]{4,3,2,1,0:T(8,128)(2,1)} %get-tuple-element.23), channel_id=1, replica_groups=mesh['dp'=16,'expert'=16] {'expert'}, dimensions={0} | all-to-all | bytes 2097152 | tf_op jit(solution)/shard_map/all_to_all | solution.py:213
  39.2 2.3 %lay_rows.1.refs_1_ = bf16[4,16,8320]{2,1,0:T(8,128)(2,1)} custom-call(bf16[16,2,4,16,256]{4,3,2,1,0:T(8,128)(2,1)} %all_to_all.10.slots_ref, bf16[4,16,128]{2,1,0:T(8,128)(2,1)} %get-tuple-element.24.meta_ref), custom_call_target="tpu_custom_call" | custom-call | tf_op jit(solution)/shard_map/lay_rows/pallas_call | solution.py:214
  41.5 1.5 collective-permute-start
  43.0 0.5 collective-permute-start.3
  43.5 3.0 %collective-permute-start.1 = (bf16[4,16,8320]{2,1,0:T(8,128)(2,1)}, bf16[4,16,8320]{2,1,0:T(8,128)(2,1)}, u32[]{:S(2)}, u32[]{:S(2)}) collective-permute-start(bf16[4,16,8320]{2,1,0:T(8,128)(2,1)} %lay_rows.1.refs_1_), channel_id=1, source_target_pairs={{0,192},{16,208},{32,224},{48,240},{64,0},{80,16},{96,32},{112,48}... | collective-permute-start | bytes 3194888 | tf_op jit(solution)/shard_map/ppermute | solution.py:182
  46.6 21.0 %collective-permute-done.refs_2_ = bf16[4,16,8320]{2,1,0:T(8,128)(2,1)} collective-permute-done((bf16[4,16,8320]{2,1,0:T(8,128)(2,1)}, bf16[4,16,8320]{2,1,0:T(8,128)(2,1)}, u32[]{:S(2)}, u32[]{:S(2)}) %collective-permute-start) | collective-permute-done | bytes 1064992 | tf_op jit(solution)/shard_map/ppermute | solution.py:182
  67.5 1.6 collective-permute-start.5
  69.1 0.2 collective-permute-done.3.refs_3_
  69.3 3.0 %collective-permute-start.4 = (bf16[4,16,8320]{2,1,0:T(8,128)(2,1)}, bf16[4,16,8320]{2,1,0:T(8,128)(2,1)}, u32[]{:S(2)}, u32[]{:S(2)}) collective-permute-start(bf16[4,16,8320]{2,1,0:T(8,128)(2,1)} %collective-permute-done.3.refs_3_), channel_id=1, source_target_pairs={{0,192},{16,208},{32,224},{48,240},{64,0},{80,16},{96,32},{112,48}... | collective-permute-start | bytes 3194888 | tf_op jit(solution)/shard_map/ppermute | solution.py:182
  72.3 1.2 collective-permute-start.2
  73.5 0.9 collective-permute-done.6.refs_4_
  74.5 1.7 %collective-permute-start.10 = (bf16[4,16,8320]{2,1,0:T(8,128)(2,1)}, bf16[4,16,8320]{2,1,0:T(8,128)(2,1)}, u32[]{:S(2)}, u32[]{:S(2)}) collective-permute-start(bf16[4,16,8320]{2,1,0:T(8,128)(2,1)} %collective-permute-done.6.refs_4_), channel_id=1, source_target_pairs={{0,48},{16,0},{32,16},{48,32},{64,112},{80,64},{96,80},{112,96},{1... | collective-permute-start | bytes 3194888 | tf_op jit(solution)/shard_map/ppermute | solution.py:182
  76.2 1.9 %copy-done.1 = bf16[1,4096,400]{1,2,0:T(8,128)(2,1)S(1)} copy-done((bf16[1,4096,400]{1,2,0:T(8,128)(2,1)S(1)}, bf16[1,4096,400]{1,2,0:T(8,128)(2,1)}, u32[]{:S(2)}) %copy-start.1) | copy-done | bytes 3276824
  78.1 1.9 %copy-done.3 = bf16[1,400,4096]{2,1,0:T(8,128)(2,1)S(1)} copy-done((bf16[1,400,4096]{2,1,0:T(8,128)(2,1)S(1)}, bf16[1,400,4096]{2,1,0:T(8,128)(2,1)}, u32[]{:S(2)}) %copy-start.3) | copy-done | bytes 3276824
  80.1 1.2 copy-done.5
  81.3 1.2 copy-done.7
  82.5 9.0 %expert_step.4.refs_10_ = f32[16,96,128]{2,1,0:T(8,128)S(1)} custom-call(s32[1]{0:T(128)} %bitcast.refs_0_, bf16[4,16,8320]{2,1,0:T(8,128)(2,1)S(1)} %copy-done.7, bf16[4,16,8320]{2,1,0:T(8,128)(2,1)} %collective-permute-done.refs_2_, bf16[4,16,8320]{2,1,0:T(8,128)(2,1)} %collective-permute-done.3.refs_3_, ...), custom_call_target="tpu_custom_call" | custom-call | flops 3145728000 | bytes 9830400 | tf_op jit(solution)/shard_map/expert_step/pallas_call | solution.py:154
  91.5 5.7 %collective-permute-done.5.refs_1_ = bf16[4,16,8320]{2,1,0:T(8,128)(2,1)} collective-permute-done((bf16[4,16,8320]{2,1,0:T(8,128)(2,1)}, bf16[4,16,8320]{2,1,0:T(8,128)(2,1)}, u32[]{:S(2)}, u32[]{:S(2)}) %collective-permute-start.5) | collective-permute-done | bytes 1064992 | tf_op jit(solution)/shard_map/ppermute | solution.py:182
  97.2 1.5 collective-permute-start.9
  98.7 1.4 collective-permute-start.8
  100.0 3.1 %collective-permute-start.7 = (bf16[4,16,8320]{2,1,0:T(8,128)(2,1)}, bf16[4,16,8320]{2,1,0:T(8,128)(2,1)S(1)}, u32[]{:S(2)}, u32[]{:S(2)}) collective-permute-start(bf16[4,16,8320]{2,1,0:T(8,128)(2,1)} %collective-permute-done.2.refs_3_), channel_id=1, source_target_pairs={{0,192},{16,208},{32,224},{48,240},{64,0},{80,16},{96,32},{112,48}... | collective-permute-start | bytes 3194888 | tf_op jit(solution)/shard_map/ppermute | solution.py:182
  103.1 1.2 slice.33
  104.3 1.1 slice.35
  105.4 1.1 slice.34
  106.5 1.1 slice.32
  107.6 7.7 %expert_step.5.refs_10_ = f32[16,96,128]{2,1,0:T(8,128)S(1)} custom-call(s32[1]{0:T(128)} %bitcast.refs_0_, bf16[4,16,8320]{2,1,0:T(8,128)(2,1)} %collective-permute-done.5.refs_1_, bf16[4,16,8320]{2,1,0:T(8,128)(2,1)} %collective-permute-done.4.refs_2_, bf16[4,16,8320]{2,1,0:T(8,128)(2,1)} %collective-permute-done.2.refs_3_, ...), custom_call_target="tpu_custom_call", output_to_operand_aliasing={{}: (10, {})} | custom-call | flops 2516582400 | bytes 9830400 | tf_op jit(solution)/shard_map/expert_step/pallas_call | solution.py:154
  115.3 7.5 %collective-permute-done.9.refs_1_ = bf16[4,16,8320]{2,1,0:T(8,128)(2,1)S(1)} collective-permute-done((bf16[4,16,8320]{2,1,0:T(8,128)(2,1)}, bf16[4,16,8320]{2,1,0:T(8,128)(2,1)S(1)}, u32[]{:S(2)}, u32[]{:S(2)}) %collective-permute-start.9) | collective-permute-done | bytes 1064992 | tf_op jit(solution)/shard_map/ppermute | solution.py:182
  122.8 1.2 collective-permute-done.8.refs_2_
  124.0 1.3 collective-permute-done.7.refs_3_
  125.3 3.3 %collective-permute-done.12.refs_4_ = bf16[4,16,8320]{2,1,0:T(8,128)(2,1)S(1)} collective-permute-done((bf16[4,16,8320]{2,1,0:T(8,128)(2,1)}, bf16[4,16,8320]{2,1,0:T(8,128)(2,1)S(1)}, u32[]{:S(2)}, u32[]{:S(2)}) %collective-permute-start.12) | collective-permute-done | bytes 1064992 | tf_op jit(solution)/shard_map/ppermute | solution.py:182
  128.7 0.1 pad_maximum_fusion.1
  128.8 0.7 collective-permute-start.13
  129.5 0.1 pad_maximum_fusion.3
  129.6 0.4 collective-permute-start.15
  130.0 0.1 pad_maximum_fusion.2
  130.1 1.8 %collective-permute-start.14 = (bf16[3,16,8320]{2,1,0:T(8,128)(2,1)S(1)}, bf16[3,16,8320]{2,1,0:T(8,128)(2,1)S(1)}, u32[]{:S(2)}, u32[]{:S(2)}) collective-permute-start(bf16[3,16,8320]{2,1,0:T(8,128)(2,1)S(1)} %pad_maximum_fusion.2), channel_id=1, source_target_pairs={{0,64},{16,80},{32,96},{48,112},{64,128},{80,144},{96,160},{112,17... | collective-permute-start | bytes 2396168 | tf_op jit(solution)/shard_map/ppermute | solution.py:182
  131.9 0.1 pad_maximum_fusion
  132.0 1.7 %collective-permute-start.11 = (bf16[3,16,8320]{2,1,0:T(8,128)(2,1)S(1)}, bf16[3,16,8320]{2,1,0:T(8,128)(2,1)S(1)}, u32[]{:S(2)}, u32[]{:S(2)}) collective-permute-start(bf16[3,16,8320]{2,1,0:T(8,128)(2,1)S(1)} %pad_maximum_fusion), channel_id=1, source_target_pairs={{0,16},{16,32},{32,48},{48,0},{64,80},{80,96},{96,112},{112,64},{1... | collective-permute-start | bytes 2396168 | tf_op jit(solution)/shard_map/ppermute | solution.py:182
  133.8 5.5 %expert_step.6.refs_10_ = f32[16,96,128]{2,1,0:T(8,128)S(1)} custom-call(s32[1]{0:T(128)} %bitcast.refs_0_, bf16[4,16,8320]{2,1,0:T(8,128)(2,1)S(1)} %collective-permute-done.9.refs_1_, bf16[4,16,8320]{2,1,0:T(8,128)(2,1)S(1)} %collective-permute-done.8.refs_2_, ...), custom_call_target="tpu_custom_call", output_to_operand_aliasing={{}: (10, {})} | custom-call | flops 2516582400 | bytes 9830400 | tf_op jit(solution)/shard_map/expert_step/pallas_call | solution.py:154
  139.2 7.1 %collective-permute-done.13.refs_2_ = bf16[3,16,8320]{2,1,0:T(8,128)(2,1)S(1)} collective-permute-done((bf16[3,16,8320]{2,1,0:T(8,128)(2,1)S(1)}, bf16[3,16,8320]{2,1,0:T(8,128)(2,1)S(1)}, u32[]{:S(2)}, u32[]{:S(2)}) %collective-permute-start.13) | collective-permute-done | bytes 798752 | tf_op jit(solution)/shard_map/ppermute | solution.py:182
  146.4 0.7 collective-permute-done.15.refs_4_
  147.0 1.7 collective-permute-done.14.refs_3_
  148.7 0.4 collective-permute-done.11.refs_1_
  149.2 4.9 %expert_step.7 = f32[16,96,128]{2,1,0:T(8,128)S(1)} custom-call(s32[1]{0:T(128)} %bitcast.refs_0_, bf16[3,16,8320]{2,1,0:T(8,128)(2,1)S(1)} %collective-permute-done.11.refs_1_, bf16[3,16,8320]{2,1,0:T(8,128)(2,1)S(1)} %collective-permute-done.13.refs_2_, bf16[3,16,8320]{2,1,0:T(8,128)(2,1)S(1)} %collective-permute-done.14.refs_3_, ...), custom_call_target="tpu_custom_call", output_to_operand_aliasing={{}: (10, {})} | custom-call | flops 1887436800 | bytes 9830400 | tf_op jit(solution)/shard_map/expert_step/pallas_call | solution.py:154
  154.1 0.5 copy.15
  154.6 16.0 %all_to_all.11 = f32[16,6,16,128]{3,2,1,0:T(8,128)S(1)} all-to-all(f32[16,6,16,128]{3,2,1,0:T(8,128)S(1)} %bitcast.23), channel_id=1, replica_groups=mesh['dp'=16,'expert'=16] {'dp'}, dimensions={0} | all-to-all | bytes 1572864 | tf_op jit(solution)/shard_map/all_to_all | solution.py:250
  170.7 0.7 reshape.16
  (26 shorter events, 0.2 us)
Async XLA Ops:
  3.0 73.2 %copy-start = (bf16[1,4096,400]{1,2,0:T(8,128)(2,1)S(1)}, bf16[1,4096,400]{1,2,0:T(8,128)(2,1)}, u32[]{:S(2)}) copy-start(bf16[1,4096,400]{1,2,0:T(8,128)(2,1)} %param.13) | copy-start | bytes 9830404
  39.2 37.0 %copy-start.8 = (bf16[400,192]{0,1:T(8,128)(2,1)S(1)}, bf16[400,192]{0,1:T(8,128)(2,1)}, u32[]{:S(2)}) copy-start(bf16[400,192]{0,1:T(8,128)(2,1)} %param.17) | copy-start | bytes 460804
  41.5 26.0 %collective-permute-start = (bf16[4,16,8320]{2,1,0:T(8,128)(2,1)}, bf16[4,16,8320]{2,1,0:T(8,128)(2,1)}, u32[]{:S(2)}, u32[]{:S(2)}) collective-permute-start(bf16[4,16,8320]{2,1,0:T(8,128)(2,1)} %lay_rows.1.refs_1_), channel_id=1, source_target_pairs={{0,16},{16,32},{32,48},{48,0},{64,80},{80,96},{96,112},{112,64},{1... | collective-permute-start | bytes 3194888 | tf_op jit(solution)/shard_map/ppermute | solution.py:182
  43.0 26.3 %collective-permute-start.3 = (bf16[4,16,8320]{2,1,0:T(8,128)(2,1)}, bf16[4,16,8320]{2,1,0:T(8,128)(2,1)}, u32[]{:S(2)}, u32[]{:S(2)}) collective-permute-start(bf16[4,16,8320]{2,1,0:T(8,128)(2,1)} %lay_rows.1.refs_1_), channel_id=1, source_target_pairs={{0,48},{16,0},{32,16},{48,32},{64,112},{80,64},{96,80},{112,96},{1... | collective-permute-start | bytes 3194888 | tf_op jit(solution)/shard_map/ppermute | solution.py:182
  43.5 28.8 %collective-permute-start.1 = (bf16[4,16,8320]{2,1,0:T(8,128)(2,1)}, bf16[4,16,8320]{2,1,0:T(8,128)(2,1)}, u32[]{:S(2)}, u32[]{:S(2)}) collective-permute-start(bf16[4,16,8320]{2,1,0:T(8,128)(2,1)} %lay_rows.1.refs_1_), channel_id=1, source_target_pairs={{0,192},{16,208},{32,224},{48,240},{64,0},{80,16},{96,32},{112,48}... | collective-permute-start | bytes 3194888 | tf_op jit(solution)/shard_map/ppermute | solution.py:182
  46.6 27.9 %collective-permute-start.6 = (bf16[4,16,8320]{2,1,0:T(8,128)(2,1)}, bf16[4,16,8320]{2,1,0:T(8,128)(2,1)}, u32[]{:S(2)}, u32[]{:S(2)}) collective-permute-start(bf16[4,16,8320]{2,1,0:T(8,128)(2,1)} %lay_rows.1.refs_1_), channel_id=1, source_target_pairs={{0,64},{16,80},{32,96},{48,112},{64,128},{80,144},{96,160},{112,17... | collective-permute-start | bytes 3194888 | tf_op jit(solution)/shard_map/ppermute | solution.py:182
  67.5 29.7 %collective-permute-start.5 = (bf16[4,16,8320]{2,1,0:T(8,128)(2,1)}, bf16[4,16,8320]{2,1,0:T(8,128)(2,1)}, u32[]{:S(2)}, u32[]{:S(2)}) collective-permute-start(bf16[4,16,8320]{2,1,0:T(8,128)(2,1)} %collective-permute-done.refs_2_), channel_id=1, source_target_pairs={{0,64},{16,80},{32,96},{48,112},{64,128},{80,144},{96,160},{112,17... | collective-permute-start | bytes 3194888 | tf_op jit(solution)/shard_map/ppermute | solution.py:182
  69.3 27.9 %collective-permute-start.4 = (bf16[4,16,8320]{2,1,0:T(8,128)(2,1)}, bf16[4,16,8320]{2,1,0:T(8,128)(2,1)}, u32[]{:S(2)}, u32[]{:S(2)}) collective-permute-start(bf16[4,16,8320]{2,1,0:T(8,128)(2,1)} %collective-permute-done.3.refs_3_), channel_id=1, source_target_pairs={{0,192},{16,208},{32,224},{48,240},{64,0},{80,16},{96,32},{112,48}... | collective-permute-start | bytes 3194888 | tf_op jit(solution)/shard_map/ppermute | solution.py:182
  72.3 26.3 %collective-permute-start.2 = (bf16[4,16,8320]{2,1,0:T(8,128)(2,1)}, bf16[4,16,8320]{2,1,0:T(8,128)(2,1)}, u32[]{:S(2)}, u32[]{:S(2)}) collective-permute-start(bf16[4,16,8320]{2,1,0:T(8,128)(2,1)} %collective-permute-done.1.refs_5_), channel_id=1, source_target_pairs={{0,16},{16,32},{32,48},{48,0},{64,80},{80,96},{96,112},{112,64},{1... | collective-permute-start | bytes 3194888 | tf_op jit(solution)/shard_map/ppermute | solution.py:182
  74.5 28.6 %collective-permute-start.10 = (bf16[4,16,8320]{2,1,0:T(8,128)(2,1)}, bf16[4,16,8320]{2,1,0:T(8,128)(2,1)}, u32[]{:S(2)}, u32[]{:S(2)}) collective-permute-start(bf16[4,16,8320]{2,1,0:T(8,128)(2,1)} %collective-permute-done.6.refs_4_), channel_id=1, source_target_pairs={{0,48},{16,0},{32,16},{48,32},{64,112},{80,64},{96,80},{112,96},{1... | collective-permute-start | bytes 3194888 | tf_op jit(solution)/shard_map/ppermute | solution.py:182
  76.2 1.9 %copy-start.1 = (bf16[1,4096,400]{1,2,0:T(8,128)(2,1)S(1)}, bf16[1,4096,400]{1,2,0:T(8,128)(2,1)}, u32[]{:S(2)}) copy-start(bf16[1,4096,400]{1,2,0:T(8,128)(2,1)} %param.14) | copy-start | bytes 9830404
  78.1 1.9 %copy-start.3 = (bf16[1,400,4096]{2,1,0:T(8,128)(2,1)S(1)}, bf16[1,400,4096]{2,1,0:T(8,128)(2,1)}, u32[]{:S(2)}) copy-start(bf16[1,400,4096]{2,1,0:T(8,128)(2,1)} %refs_7_.5) | copy-start | bytes 9830404
  80.1 1.2 copy-start.5
  81.3 1.2 copy-start.7
  82.5 25.1 %copy-start.4 = (bf16[1,400,4096]{2,1,0:T(8,128)(2,1)S(1)}, bf16[1,400,4096]{2,1,0:T(8,128)(2,1)}, u32[]{:S(2)}) copy-start(bf16[1,400,4096]{2,1,0:T(8,128)(2,1)} %refs_7_.5) | copy-start | bytes 9830404
  82.5 25.1 %copy-start.6 = (bf16[4096,128]{1,0:T(8,128)(2,1)S(1)}, bf16[4096,128]{1,0:T(8,128)(2,1)}, u32[]{:S(2)}) copy-start(bf16[4096,128]{1,0:T(8,128)(2,1)} %refs_8_.7) | copy-start | bytes 3145732
  97.2 25.6 %collective-permute-start.9 = (bf16[4,16,8320]{2,1,0:T(8,128)(2,1)}, bf16[4,16,8320]{2,1,0:T(8,128)(2,1)S(1)}, u32[]{:S(2)}, u32[]{:S(2)}) collective-permute-start(bf16[4,16,8320]{2,1,0:T(8,128)(2,1)} %collective-permute-done.5.refs_1_), channel_id=1, source_target_pairs={{0,16},{16,32},{32,48},{48,0},{64,80},{80,96},{96,112},{112,64},{1... | collective-permute-start | bytes 3194888 | tf_op jit(solution)/shard_map/ppermute | solution.py:182
  98.7 25.4 %collective-permute-start.8 = (bf16[4,16,8320]{2,1,0:T(8,128)(2,1)}, bf16[4,16,8320]{2,1,0:T(8,128)(2,1)S(1)}, u32[]{:S(2)}, u32[]{:S(2)}) collective-permute-start(bf16[4,16,8320]{2,1,0:T(8,128)(2,1)} %collective-permute-done.4.refs_2_), channel_id=1, source_target_pairs={{0,48},{16,0},{32,16},{48,32},{64,112},{80,64},{96,80},{112,96},{1... | collective-permute-start | bytes 3194888 | tf_op jit(solution)/shard_map/ppermute | solution.py:182
  100.0 25.3 %collective-permute-start.7 = (bf16[4,16,8320]{2,1,0:T(8,128)(2,1)}, bf16[4,16,8320]{2,1,0:T(8,128)(2,1)S(1)}, u32[]{:S(2)}, u32[]{:S(2)}) collective-permute-start(bf16[4,16,8320]{2,1,0:T(8,128)(2,1)} %collective-permute-done.2.refs_3_), channel_id=1, source_target_pairs={{0,192},{16,208},{32,224},{48,240},{64,0},{80,16},{96,32},{112,48}... | collective-permute-start | bytes 3194888 | tf_op jit(solution)/shard_map/ppermute | solution.py:182
  103.1 25.6 %collective-permute-start.12 = (bf16[4,16,8320]{2,1,0:T(8,128)(2,1)}, bf16[4,16,8320]{2,1,0:T(8,128)(2,1)S(1)}, u32[]{:S(2)}, u32[]{:S(2)}) collective-permute-start(bf16[4,16,8320]{2,1,0:T(8,128)(2,1)} %collective-permute-done.10.refs_4_), channel_id=1, source_target_pairs={{0,64},{16,80},{32,96},{48,112},{64,128},{80,144},{96,160},{112,17... | collective-permute-start | bytes 3194888 | tf_op jit(solution)/shard_map/ppermute | solution.py:182
  103.1 4.5 %copy-start.2 = (bf16[1,4096,400]{1,2,0:T(8,128)(2,1)S(1)}, bf16[1,4096,400]{1,2,0:T(8,128)(2,1)}, u32[]{:S(2)}) copy-start(bf16[1,4096,400]{1,2,0:T(8,128)(2,1)} %param.14) | copy-start | bytes 9830404
  128.8 17.6 %collective-permute-start.13 = (bf16[3,16,8320]{2,1,0:T(8,128)(2,1)S(1)}, bf16[3,16,8320]{2,1,0:T(8,128)(2,1)S(1)}, u32[]{:S(2)}, u32[]{:S(2)}) collective-permute-start(bf16[3,16,8320]{2,1,0:T(8,128)(2,1)S(1)} %pad_maximum_fusion.1), channel_id=1, source_target_pairs={{0,48},{16,0},{32,16},{48,32},{64,112},{80,64},{96,80},{112,96},{1... | collective-permute-start | bytes 2396168 | tf_op jit(solution)/shard_map/ppermute | solution.py:182
  129.6 17.5 %collective-permute-start.15 = (bf16[3,16,8320]{2,1,0:T(8,128)(2,1)S(1)}, bf16[3,16,8320]{2,1,0:T(8,128)(2,1)S(1)}, u32[]{:S(2)}, u32[]{:S(2)}) collective-permute-start(bf16[3,16,8320]{2,1,0:T(8,128)(2,1)S(1)} %pad_maximum_fusion.3), channel_id=1, source_target_pairs={{0,192},{16,208},{32,224},{48,240},{64,0},{80,16},{96,32},{112,48}... | collective-permute-start | bytes 2396168 | tf_op jit(solution)/shard_map/ppermute | solution.py:182
  130.1 18.7 %collective-permute-start.14 = (bf16[3,16,8320]{2,1,0:T(8,128)(2,1)S(1)}, bf16[3,16,8320]{2,1,0:T(8,128)(2,1)S(1)}, u32[]{:S(2)}, u32[]{:S(2)}) collective-permute-start(bf16[3,16,8320]{2,1,0:T(8,128)(2,1)S(1)} %pad_maximum_fusion.2), channel_id=1, source_target_pairs={{0,64},{16,80},{32,96},{48,112},{64,128},{80,144},{96,160},{112,17... | collective-permute-start | bytes 2396168 | tf_op jit(solution)/shard_map/ppermute | solution.py:182
  132.0 17.2 %collective-permute-start.11 = (bf16[3,16,8320]{2,1,0:T(8,128)(2,1)S(1)}, bf16[3,16,8320]{2,1,0:T(8,128)(2,1)S(1)}, u32[]{:S(2)}, u32[]{:S(2)}) collective-permute-start(bf16[3,16,8320]{2,1,0:T(8,128)(2,1)S(1)} %pad_maximum_fusion), channel_id=1, source_target_pairs={{0,16},{16,32},{32,48},{48,0},{64,80},{80,96},{96,112},{112,64},{1... | collective-permute-start | bytes 2396168 | tf_op jit(solution)/shard_map/ppermute | solution.py:182

commit v2 on v1

--- a/solution.py
+++ b/solution.py
@@ -247,8 +247,8 @@
     )
 
     share = acc.reshape(n_dp, n_dp, -1, LANES).transpose(1, 2, 0, 3)
-    share = lax.all_to_all(share, "dp", split_axis=0, concat_axis=0, tiled=True)
-    total = jnp.sum(share, axis=0)
+    share = lax.all_to_all(share.astype(BF16), "dp", split_axis=0, concat_axis=0, tiled=True)
+    total = jnp.sum(share.astype(F32), axis=0)
     return total.transpose(1, 0, 2).reshape(n_dp, 1, -1)
 
 

time: 172 us -> 169 us (0.983)
  blocking collectives: 52.2 us -> 50 us
    all_to_all x1, blocking collectives: 16 us -> 13.8 us  [per_device(): lax.all_to_all(share.astype(BF16), 'dp', split_axis=0, concat_axis=0, til...]
where the time goes in v2:
time: 169 us
  waiting for transfers between devices  51.1 us (30%)
  blocking collectives  50 us (30%)
  Pallas kernels  32.4 us (19%)
  starting transfers between devices  23.1 us (14%)
  local copies, waits for them, and re-layouts  11.7 us (7%)
    ppermute x16, waiting for transfers between devices, shift(): return lax.ppermute(block, 'dp', moves)  51.1 us
    all_to_all x1, blocking collectives, per_device(): lax.all_to_all(slots, 'expert', split_axis=0, concat_axis=0, tiled=True)  36.2 us
    pallas_call x4, Pallas kernels, step(): pl.pallas_call(lambda *refs: step_kernel(sources, len(bufs), first, *refs...  27.1 us
    ppermute x16, starting transfers between devices, shift(): return lax.ppermute(block, 'dp', moves)  23.1 us
    all_to_all x1, blocking collectives, per_device(): lax.all_to_all(share.astype(BF16), 'dp', split_axis=0, concat_axis=0, til...  13.8 us
    unnamed x18, local copies, waits for them, and re-layouts  6.33 us
  transfers between devices with their start and end apart: 16, of which 12 were waited for; matrix products, arithmetic and copies ran while one was open for 3% of the time, Pallas kernels for 13%

profile of v2, /device:TPU:2, one launch (start us, length us, event | category | flops | bytes accessed | tf_op | source)
XLA Modules:
  0.0 168.9 jit_solution(4249867167648061060)
XLA Ops:
  0.0 3.0 %pack_slots.1 = (bf16[16,2,4,16,256]{4,3,2,1,0:T(8,128)(2,1)}, bf16[4,16,128]{2,1,0:T(8,128)(2,1)}) custom-call(s32[1]{0:T(128)} %bitcast.1.refs_0_, s32[2,256]{1,0:T(2,128)} %bitcast.25, s32[2,256]{1,0:T(2,128)} %bitcast.26, bf16[256,256]{1,0:T(8,128)(2,1)} %refs_3_.1, bf16[256,256]{1,0:T(8,128)(2,1)} %refs_4_.1), custom_call_target="tpu_custom_call" | custom-call | tf_op jit(solution)/shard_map/pack_slots/pallas_call | solution.py:203
  3.0 36.2 %all_to_all.10.slots_ref = bf16[16,2,4,16,256]{4,3,2,1,0:T(8,128)(2,1)} all-to-all(bf16[16,2,4,16,256]{4,3,2,1,0:T(8,128)(2,1)} %get-tuple-element.23), channel_id=1, replica_groups=mesh['dp'=16,'expert'=16] {'expert'}, dimensions={0} | all-to-all | bytes 2097152 | tf_op jit(solution)/shard_map/all_to_all | solution.py:213
  39.2 2.3 %lay_rows.1.refs_1_ = bf16[4,16,8320]{2,1,0:T(8,128)(2,1)} custom-call(bf16[16,2,4,16,256]{4,3,2,1,0:T(8,128)(2,1)} %all_to_all.10.slots_ref, bf16[4,16,128]{2,1,0:T(8,128)(2,1)} %get-tuple-element.24.meta_ref), custom_call_target="tpu_custom_call" | custom-call | tf_op jit(solution)/shard_map/lay_rows/pallas_call | solution.py:214
  41.5 1.5 collective-permute-start
  43.0 0.5 collective-permute-start.3
  43.5 3.0 %collective-permute-start.1 = (bf16[4,16,8320]{2,1,0:T(8,128)(2,1)}, bf16[4,16,8320]{2,1,0:T(8,128)(2,1)}, u32[]{:S(2)}, u32[]{:S(2)}) collective-permute-start(bf16[4,16,8320]{2,1,0:T(8,128)(2,1)} %lay_rows.1.refs_1_), channel_id=1, source_target_pairs={{0,192},{16,208},{32,224},{48,240},{64,0},{80,16},{96,32},{112,48}... | collective-permute-start | bytes 3194888 | tf_op jit(solution)/shard_map/ppermute | solution.py:182
  46.6 21.0 %collective-permute-done.refs_2_ = bf16[4,16,8320]{2,1,0:T(8,128)(2,1)} collective-permute-done((bf16[4,16,8320]{2,1,0:T(8,128)(2,1)}, bf16[4,16,8320]{2,1,0:T(8,128)(2,1)}, u32[]{:S(2)}, u32[]{:S(2)}) %collective-permute-start) | collective-permute-done | bytes 1064992 | tf_op jit(solution)/shard_map/ppermute | solution.py:182
  67.5 1.6 collective-permute-start.5
  69.1 0.2 collective-permute-done.3.refs_3_
  69.3 3.0 %collective-permute-start.4 = (bf16[4,16,8320]{2,1,0:T(8,128)(2,1)}, bf16[4,16,8320]{2,1,0:T(8,128)(2,1)}, u32[]{:S(2)}, u32[]{:S(2)}) collective-permute-start(bf16[4,16,8320]{2,1,0:T(8,128)(2,1)} %collective-permute-done.3.refs_3_), channel_id=1, source_target_pairs={{0,192},{16,208},{32,224},{48,240},{64,0},{80,16},{96,32},{112,48}... | collective-permute-start | bytes 3194888 | tf_op jit(solution)/shard_map/ppermute | solution.py:182
  72.3 1.2 collective-permute-start.2
  73.5 0.9 collective-permute-done.6.refs_4_
  74.5 1.7 %collective-permute-start.10 = (bf16[4,16,8320]{2,1,0:T(8,128)(2,1)}, bf16[4,16,8320]{2,1,0:T(8,128)(2,1)}, u32[]{:S(2)}, u32[]{:S(2)}) collective-permute-start(bf16[4,16,8320]{2,1,0:T(8,128)(2,1)} %collective-permute-done.6.refs_4_), channel_id=1, source_target_pairs={{0,48},{16,0},{32,16},{48,32},{64,112},{80,64},{96,80},{112,96},{1... | collective-permute-start | bytes 3194888 | tf_op jit(solution)/shard_map/ppermute | solution.py:182
  76.2 1.9 %copy-done.1 = bf16[1,4096,400]{1,2,0:T(8,128)(2,1)S(1)} copy-done((bf16[1,4096,400]{1,2,0:T(8,128)(2,1)S(1)}, bf16[1,4096,400]{1,2,0:T(8,128)(2,1)}, u32[]{:S(2)}) %copy-start.1) | copy-done | bytes 3276824
  78.1 1.9 %copy-done.3 = bf16[1,400,4096]{2,1,0:T(8,128)(2,1)S(1)} copy-done((bf16[1,400,4096]{2,1,0:T(8,128)(2,1)S(1)}, bf16[1,400,4096]{2,1,0:T(8,128)(2,1)}, u32[]{:S(2)}) %copy-start.3) | copy-done | bytes 3276824
  80.1 1.2 copy-done.5
  81.3 1.2 copy-done.7
  82.5 9.0 %expert_step.4.refs_10_ = f32[16,96,128]{2,1,0:T(8,128)S(1)} custom-call(s32[1]{0:T(128)} %bitcast.refs_0_, bf16[4,16,8320]{2,1,0:T(8,128)(2,1)S(1)} %copy-done.7, bf16[4,16,8320]{2,1,0:T(8,128)(2,1)} %collective-permute-done.refs_2_, bf16[4,16,8320]{2,1,0:T(8,128)(2,1)} %collective-permute-done.3.refs_3_, ...), custom_call_target="tpu_custom_call" | custom-call | flops 3145728000 | bytes 9830400 | tf_op jit(solution)/shard_map/expert_step/pallas_call | solution.py:154
  91.5 5.7 %collective-permute-done.5.refs_1_ = bf16[4,16,8320]{2,1,0:T(8,128)(2,1)} collective-permute-done((bf16[4,16,8320]{2,1,0:T(8,128)(2,1)}, bf16[4,16,8320]{2,1,0:T(8,128)(2,1)}, u32[]{:S(2)}, u32[]{:S(2)}) %collective-permute-start.5) | collective-permute-done | bytes 1064992 | tf_op jit(solution)/shard_map/ppermute | solution.py:182
  97.2 1.5 collective-permute-start.9
  98.7 1.4 collective-permute-start.8
  100.0 3.1 %collective-permute-start.7 = (bf16[4,16,8320]{2,1,0:T(8,128)(2,1)}, bf16[4,16,8320]{2,1,0:T(8,128)(2,1)S(1)}, u32[]{:S(2)}, u32[]{:S(2)}) collective-permute-start(bf16[4,16,8320]{2,1,0:T(8,128)(2,1)} %collective-permute-done.2.refs_3_), channel_id=1, source_target_pairs={{0,192},{16,208},{32,224},{48,240},{64,0},{80,16},{96,32},{112,48}... | collective-permute-start | bytes 3194888 | tf_op jit(solution)/shard_map/ppermute | solution.py:182
  103.1 1.2 slice.33
  104.3 1.1 slice.35
  105.4 1.1 slice.34
  106.5 1.1 slice.32
  107.6 7.7 %expert_step.5.refs_10_ = f32[16,96,128]{2,1,0:T(8,128)S(1)} custom-call(s32[1]{0:T(128)} %bitcast.refs_0_, bf16[4,16,8320]{2,1,0:T(8,128)(2,1)} %collective-permute-done.5.refs_1_, bf16[4,16,8320]{2,1,0:T(8,128)(2,1)} %collective-permute-done.4.refs_2_, bf16[4,16,8320]{2,1,0:T(8,128)(2,1)} %collective-permute-done.2.refs_3_, ...), custom_call_target="tpu_custom_call", output_to_operand_aliasing={{}: (10, {})} | custom-call | flops 2516582400 | bytes 9830400 | tf_op jit(solution)/shard_map/expert_step/pallas_call | solution.py:154
  115.3 7.5 %collective-permute-done.9.refs_1_ = bf16[4,16,8320]{2,1,0:T(8,128)(2,1)S(1)} collective-permute-done((bf16[4,16,8320]{2,1,0:T(8,128)(2,1)}, bf16[4,16,8320]{2,1,0:T(8,128)(2,1)S(1)}, u32[]{:S(2)}, u32[]{:S(2)}) %collective-permute-start.9) | collective-permute-done | bytes 1064992 | tf_op jit(solution)/shard_map/ppermute | solution.py:182
  122.8 1.2 collective-permute-done.8.refs_2_
  124.0 1.3 collective-permute-done.7.refs_3_
  125.3 3.3 %collective-permute-done.12.refs_4_ = bf16[4,16,8320]{2,1,0:T(8,128)(2,1)S(1)} collective-permute-done((bf16[4,16,8320]{2,1,0:T(8,128)(2,1)}, bf16[4,16,8320]{2,1,0:T(8,128)(2,1)S(1)}, u32[]{:S(2)}, u32[]{:S(2)}) %collective-permute-start.12) | collective-permute-done | bytes 1064992 | tf_op jit(solution)/shard_map/ppermute | solution.py:182
  128.7 0.1 pad_maximum_fusion.1
  128.8 0.7 collective-permute-start.13
  129.5 0.1 pad_maximum_fusion.3
  129.6 0.4 collective-permute-start.15
  130.0 0.1 pad_maximum_fusion.2
  130.1 1.8 %collective-permute-start.14 = (bf16[3,16,8320]{2,1,0:T(8,128)(2,1)S(1)}, bf16[3,16,8320]{2,1,0:T(8,128)(2,1)S(1)}, u32[]{:S(2)}, u32[]{:S(2)}) collective-permute-start(bf16[3,16,8320]{2,1,0:T(8,128)(2,1)S(1)} %pad_maximum_fusion.2), channel_id=1, source_target_pairs={{0,64},{16,80},{32,96},{48,112},{64,128},{80,144},{96,160},{112,17... | collective-permute-start | bytes 2396168 | tf_op jit(solution)/shard_map/ppermute | solution.py:182
  131.9 0.1 pad_maximum_fusion
  132.0 1.7 %collective-permute-start.11 = (bf16[3,16,8320]{2,1,0:T(8,128)(2,1)S(1)}, bf16[3,16,8320]{2,1,0:T(8,128)(2,1)S(1)}, u32[]{:S(2)}, u32[]{:S(2)}) collective-permute-start(bf16[3,16,8320]{2,1,0:T(8,128)(2,1)S(1)} %pad_maximum_fusion), channel_id=1, source_target_pairs={{0,16},{16,32},{32,48},{48,0},{64,80},{80,96},{96,112},{112,64},{1... | collective-permute-start | bytes 2396168 | tf_op jit(solution)/shard_map/ppermute | solution.py:182
  133.8 5.5 %expert_step.6.refs_10_ = f32[16,96,128]{2,1,0:T(8,128)S(1)} custom-call(s32[1]{0:T(128)} %bitcast.refs_0_, bf16[4,16,8320]{2,1,0:T(8,128)(2,1)S(1)} %collective-permute-done.9.refs_1_, bf16[4,16,8320]{2,1,0:T(8,128)(2,1)S(1)} %collective-permute-done.8.refs_2_, ...), custom_call_target="tpu_custom_call", output_to_operand_aliasing={{}: (10, {})} | custom-call | flops 2516582400 | bytes 9830400 | tf_op jit(solution)/shard_map/expert_step/pallas_call | solution.py:154
  139.2 7.1 %collective-permute-done.13.refs_2_ = bf16[3,16,8320]{2,1,0:T(8,128)(2,1)S(1)} collective-permute-done((bf16[3,16,8320]{2,1,0:T(8,128)(2,1)S(1)}, bf16[3,16,8320]{2,1,0:T(8,128)(2,1)S(1)}, u32[]{:S(2)}, u32[]{:S(2)}) %collective-permute-start.13) | collective-permute-done | bytes 798752 | tf_op jit(solution)/shard_map/ppermute | solution.py:182
  146.4 0.7 collective-permute-done.15.refs_4_
  147.0 1.7 collective-permute-done.14.refs_3_
  148.7 0.4 collective-permute-done.11.refs_1_
  149.2 4.9 %expert_step.7 = f32[16,96,128]{2,1,0:T(8,128)S(1)} custom-call(s32[1]{0:T(128)} %bitcast.refs_0_, bf16[3,16,8320]{2,1,0:T(8,128)(2,1)S(1)} %collective-permute-done.11.refs_1_, bf16[3,16,8320]{2,1,0:T(8,128)(2,1)S(1)} %collective-permute-done.13.refs_2_, bf16[3,16,8320]{2,1,0:T(8,128)(2,1)S(1)} %collective-permute-done.14.refs_3_, ...), custom_call_target="tpu_custom_call", output_to_operand_aliasing={{}: (10, {})} | custom-call | flops 1887436800 | bytes 9830400 | tf_op jit(solution)/shard_map/expert_step/pallas_call | solution.py:154
  154.2 0.2 copy.15
  154.3 13.8 %all_to_all.11 = bf16[16,6,16,128]{3,2,1,0:T(8,128)(2,1)S(1)} all-to-all(bf16[16,6,16,128]{3,2,1,0:T(8,128)(2,1)S(1)} %bitcast.23), channel_id=1, replica_groups=mesh['dp'=16,'expert'=16] {'dp'}, dimensions={0} | all-to-all | bytes 786432 | tf_op jit(solution)/shard_map/all_to_all | solution.py:250
  168.3 0.7 reshape.14
  (27 shorter events, 0.2 us)
Async XLA Ops:
  3.0 73.2 %copy-start = (bf16[1,4096,400]{1,2,0:T(8,128)(2,1)S(1)}, bf16[1,4096,400]{1,2,0:T(8,128)(2,1)}, u32[]{:S(2)}) copy-start(bf16[1,4096,400]{1,2,0:T(8,128)(2,1)} %param.13) | copy-start | bytes 9830404
  39.2 37.0 %copy-start.8 = (bf16[400,192]{0,1:T(8,128)(2,1)S(1)}, bf16[400,192]{0,1:T(8,128)(2,1)}, u32[]{:S(2)}) copy-start(bf16[400,192]{0,1:T(8,128)(2,1)} %param.17) | copy-start | bytes 460804
  41.5 26.0 %collective-permute-start = (bf16[4,16,8320]{2,1,0:T(8,128)(2,1)}, bf16[4,16,8320]{2,1,0:T(8,128)(2,1)}, u32[]{:S(2)}, u32[]{:S(2)}) collective-permute-start(bf16[4,16,8320]{2,1,0:T(8,128)(2,1)} %lay_rows.1.refs_1_), channel_id=1, source_target_pairs={{0,16},{16,32},{32,48},{48,0},{64,80},{80,96},{96,112},{112,64},{1... | collective-permute-start | bytes 3194888 | tf_op jit(solution)/shard_map/ppermute | solution.py:182
  43.0 26.3 %collective-permute-start.3 = (bf16[4,16,8320]{2,1,0:T(8,128)(2,1)}, bf16[4,16,8320]{2,1,0:T(8,128)(2,1)}, u32[]{:S(2)}, u32[]{:S(2)}) collective-permute-start(bf16[4,16,8320]{2,1,0:T(8,128)(2,1)} %lay_rows.1.refs_1_), channel_id=1, source_target_pairs={{0,48},{16,0},{32,16},{48,32},{64,112},{80,64},{96,80},{112,96},{1... | collective-permute-start | bytes 3194888 | tf_op jit(solution)/shard_map/ppermute | solution.py:182
  43.5 28.8 %collective-permute-start.1 = (bf16[4,16,8320]{2,1,0:T(8,128)(2,1)}, bf16[4,16,8320]{2,1,0:T(8,128)(2,1)}, u32[]{:S(2)}, u32[]{:S(2)}) collective-permute-start(bf16[4,16,8320]{2,1,0:T(8,128)(2,1)} %lay_rows.1.refs_1_), channel_id=1, source_target_pairs={{0,192},{16,208},{32,224},{48,240},{64,0},{80,16},{96,32},{112,48}... | collective-permute-start | bytes 3194888 | tf_op jit(solution)/shard_map/ppermute | solution.py:182
  46.6 27.9 %collective-permute-start.6 = (bf16[4,16,8320]{2,1,0:T(8,128)(2,1)}, bf16[4,16,8320]{2,1,0:T(8,128)(2,1)}, u32[]{:S(2)}, u32[]{:S(2)}) collective-permute-start(bf16[4,16,8320]{2,1,0:T(8,128)(2,1)} %lay_rows.1.refs_1_), channel_id=1, source_target_pairs={{0,64},{16,80},{32,96},{48,112},{64,128},{80,144},{96,160},{112,17... | collective-permute-start | bytes 3194888 | tf_op jit(solution)/shard_map/ppermute | solution.py:182
  67.5 29.7 %collective-permute-start.5 = (bf16[4,16,8320]{2,1,0:T(8,128)(2,1)}, bf16[4,16,8320]{2,1,0:T(8,128)(2,1)}, u32[]{:S(2)}, u32[]{:S(2)}) collective-permute-start(bf16[4,16,8320]{2,1,0:T(8,128)(2,1)} %collective-permute-done.refs_2_), channel_id=1, source_target_pairs={{0,64},{16,80},{32,96},{48,112},{64,128},{80,144},{96,160},{112,17... | collective-permute-start | bytes 3194888 | tf_op jit(solution)/shard_map/ppermute | solution.py:182
  69.3 27.9 %collective-permute-start.4 = (bf16[4,16,8320]{2,1,0:T(8,128)(2,1)}, bf16[4,16,8320]{2,1,0:T(8,128)(2,1)}, u32[]{:S(2)}, u32[]{:S(2)}) collective-permute-start(bf16[4,16,8320]{2,1,0:T(8,128)(2,1)} %collective-permute-done.3.refs_3_), channel_id=1, source_target_pairs={{0,192},{16,208},{32,224},{48,240},{64,0},{80,16},{96,32},{112,48}... | collective-permute-start | bytes 3194888 | tf_op jit(solution)/shard_map/ppermute | solution.py:182
  72.3 26.3 %collective-permute-start.2 = (bf16[4,16,8320]{2,1,0:T(8,128)(2,1)}, bf16[4,16,8320]{2,1,0:T(8,128)(2,1)}, u32[]{:S(2)}, u32[]{:S(2)}) collective-permute-start(bf16[4,16,8320]{2,1,0:T(8,128)(2,1)} %collective-permute-done.1.refs_5_), channel_id=1, source_target_pairs={{0,16},{16,32},{32,48},{48,0},{64,80},{80,96},{96,112},{112,64},{1... | collective-permute-start | bytes 3194888 | tf_op jit(solution)/shard_map/ppermute | solution.py:182
  74.5 28.6 %collective-permute-start.10 = (bf16[4,16,8320]{2,1,0:T(8,128)(2,1)}, bf16[4,16,8320]{2,1,0:T(8,128)(2,1)}, u32[]{:S(2)}, u32[]{:S(2)}) collective-permute-start(bf16[4,16,8320]{2,1,0:T(8,128)(2,1)} %collective-permute-done.6.refs_4_), channel_id=1, source_target_pairs={{0,48},{16,0},{32,16},{48,32},{64,112},{80,64},{96,80},{112,96},{1... | collective-permute-start | bytes 3194888 | tf_op jit(solution)/shard_map/ppermute | solution.py:182
  76.2 1.9 %copy-start.1 = (bf16[1,4096,400]{1,2,0:T(8,128)(2,1)S(1)}, bf16[1,4096,400]{1,2,0:T(8,128)(2,1)}, u32[]{:S(2)}) copy-start(bf16[1,4096,400]{1,2,0:T(8,128)(2,1)} %param.14) | copy-start | bytes 9830404
  78.1 1.9 %copy-start.3 = (bf16[1,400,4096]{2,1,0:T(8,128)(2,1)S(1)}, bf16[1,400,4096]{2,1,0:T(8,128)(2,1)}, u32[]{:S(2)}) copy-start(bf16[1,400,4096]{2,1,0:T(8,128)(2,1)} %refs_7_.5) | copy-start | bytes 9830404
  80.1 1.2 copy-start.5
  81.3 1.2 copy-start.7
  82.5 25.1 %copy-start.4 = (bf16[1,400,4096]{2,1,0:T(8,128)(2,1)S(1)}, bf16[1,400,4096]{2,1,0:T(8,128)(2,1)}, u32[]{:S(2)}) copy-start(bf16[1,400,4096]{2,1,0:T(8,128)(2,1)} %refs_7_.5) | copy-start | bytes 9830404
  82.5 25.1 %copy-start.6 = (bf16[4096,128]{1,0:T(8,128)(2,1)S(1)}, bf16[4096,128]{1,0:T(8,128)(2,1)}, u32[]{:S(2)}) copy-start(bf16[4096,128]{1,0:T(8,128)(2,1)} %refs_8_.7) | copy-start | bytes 3145732
  97.2 25.6 %collective-permute-start.9 = (bf16[4,16,8320]{2,1,0:T(8,128)(2,1)}, bf16[4,16,8320]{2,1,0:T(8,128)(2,1)S(1)}, u32[]{:S(2)}, u32[]{:S(2)}) collective-permute-start(bf16[4,16,8320]{2,1,0:T(8,128)(2,1)} %collective-permute-done.5.refs_1_), channel_id=1, source_target_pairs={{0,16},{16,32},{32,48},{48,0},{64,80},{80,96},{96,112},{112,64},{1... | collective-permute-start | bytes 3194888 | tf_op jit(solution)/shard_map/ppermute | solution.py:182
  98.7 25.4 %collective-permute-start.8 = (bf16[4,16,8320]{2,1,0:T(8,128)(2,1)}, bf16[4,16,8320]{2,1,0:T(8,128)(2,1)S(1)}, u32[]{:S(2)}, u32[]{:S(2)}) collective-permute-start(bf16[4,16,8320]{2,1,0:T(8,128)(2,1)} %collective-permute-done.4.refs_2_), channel_id=1, source_target_pairs={{0,48},{16,0},{32,16},{48,32},{64,112},{80,64},{96,80},{112,96},{1... | collective-permute-start | bytes 3194888 | tf_op jit(solution)/shard_map/ppermute | solution.py:182
  100.0 25.3 %collective-permute-start.7 = (bf16[4,16,8320]{2,1,0:T(8,128)(2,1)}, bf16[4,16,8320]{2,1,0:T(8,128)(2,1)S(1)}, u32[]{:S(2)}, u32[]{:S(2)}) collective-permute-start(bf16[4,16,8320]{2,1,0:T(8,128)(2,1)} %collective-permute-done.2.refs_3_), channel_id=1, source_target_pairs={{0,192},{16,208},{32,224},{48,240},{64,0},{80,16},{96,32},{112,48}... | collective-permute-start | bytes 3194888 | tf_op jit(solution)/shard_map/ppermute | solution.py:182
  103.1 25.6 %collective-permute-start.12 = (bf16[4,16,8320]{2,1,0:T(8,128)(2,1)}, bf16[4,16,8320]{2,1,0:T(8,128)(2,1)S(1)}, u32[]{:S(2)}, u32[]{:S(2)}) collective-permute-start(bf16[4,16,8320]{2,1,0:T(8,128)(2,1)} %collective-permute-done.10.refs_4_), channel_id=1, source_target_pairs={{0,64},{16,80},{32,96},{48,112},{64,128},{80,144},{96,160},{112,17... | collective-permute-start | bytes 3194888 | tf_op jit(solution)/shard_map/ppermute | solution.py:182
  103.1 4.5 %copy-start.2 = (bf16[1,4096,400]{1,2,0:T(8,128)(2,1)S(1)}, bf16[1,4096,400]{1,2,0:T(8,128)(2,1)}, u32[]{:S(2)}) copy-start(bf16[1,4096,400]{1,2,0:T(8,128)(2,1)} %param.14) | copy-start | bytes 9830404
  128.8 17.6 %collective-permute-start.13 = (bf16[3,16,8320]{2,1,0:T(8,128)(2,1)S(1)}, bf16[3,16,8320]{2,1,0:T(8,128)(2,1)S(1)}, u32[]{:S(2)}, u32[]{:S(2)}) collective-permute-start(bf16[3,16,8320]{2,1,0:T(8,128)(2,1)S(1)} %pad_maximum_fusion.1), channel_id=1, source_target_pairs={{0,48},{16,0},{32,16},{48,32},{64,112},{80,64},{96,80},{112,96},{1... | collective-permute-start | bytes 2396168 | tf_op jit(solution)/shard_map/ppermute | solution.py:182
  129.6 17.5 %collective-permute-start.15 = (bf16[3,16,8320]{2,1,0:T(8,128)(2,1)S(1)}, bf16[3,16,8320]{2,1,0:T(8,128)(2,1)S(1)}, u32[]{:S(2)}, u32[]{:S(2)}) collective-permute-start(bf16[3,16,8320]{2,1,0:T(8,128)(2,1)S(1)} %pad_maximum_fusion.3), channel_id=1, source_target_pairs={{0,192},{16,208},{32,224},{48,240},{64,0},{80,16},{96,32},{112,48}... | collective-permute-start | bytes 2396168 | tf_op jit(solution)/shard_map/ppermute | solution.py:182
  130.1 18.7 %collective-permute-start.14 = (bf16[3,16,8320]{2,1,0:T(8,128)(2,1)S(1)}, bf16[3,16,8320]{2,1,0:T(8,128)(2,1)S(1)}, u32[]{:S(2)}, u32[]{:S(2)}) collective-permute-start(bf16[3,16,8320]{2,1,0:T(8,128)(2,1)S(1)} %pad_maximum_fusion.2), channel_id=1, source_target_pairs={{0,64},{16,80},{32,96},{48,112},{64,128},{80,144},{96,160},{112,17... | collective-permute-start | bytes 2396168 | tf_op jit(solution)/shard_map/ppermute | solution.py:182
  132.0 17.2 %collective-permute-start.11 = (bf16[3,16,8320]{2,1,0:T(8,128)(2,1)S(1)}, bf16[3,16,8320]{2,1,0:T(8,128)(2,1)S(1)}, u32[]{:S(2)}, u32[]{:S(2)}) collective-permute-start(bf16[3,16,8320]{2,1,0:T(8,128)(2,1)S(1)} %pad_maximum_fusion), channel_id=1, source_target_pairs={{0,16},{16,32},{32,48},{48,0},{64,80},{80,96},{96,112},{112,64},{1... | collective-permute-start | bytes 2396168 | tf_op jit(solution)/shard_map/ppermute | solution.py:182
